TPU v7x, 256 devices: a whole 4x4x8 slice. The times are simulated.
256 devices in a mesh: section: 16 (over x, y), dp: 8 (over z), tensor: 2 (over core).
Axes of the slice: x: 4, y: 4, z: 8, core: 2. Of those that a mesh axis runs over, the one named last changes fastest.
Arguments:
- hidden: bfloat16 [8, 128, 3584], P('dp', 'section', 'tensor'), may hold values from -14 to 14
- head_weight: bfloat16 [3584, 81920], P('tensor', ('section', 'dp')), may hold values from -3 to 3
- teacher_logprobs: float32 [8, 128, 81920], P(None, 'tensor', ('section', 'dp')), may hold values from -40 to 4
- lengths: int32 [8, 4], replicated, may hold values from 1 to 32, 80 in all within a row
Outputs:
- hidden_grad: bfloat16 [8, 128, 3584], P('dp', 'section', 'tensor')
- divergence: float32 [8, 128], P('dp', 'tensor')
Inputs may be any that keep to these rules, and one draw needn't show every extreme that they name: Each replica's 4 lengths sum to 80.
All inputs are finite; a program needn't handle non-finite values.
Results may differ from a plain program's by a relative error of at most 0.0051.
Values may be sent and summed in bfloat16 or wider, within the bound.
A program may use at most 64 MiB of HBM per device.

v0:
```python
import jax
import jax.numpy as jnp
from jax import lax
from jax.sharding import PartitionSpec as P

SEQ_MB = 32


def row_weights(lengths, replica, positions, seq_len):
    micro_index = positions // seq_len
    within_index = positions % seq_len
    replica_pick = (
        replica[:, None] == jnp.arange(lengths.shape[0], dtype=jnp.int32)[None, :]
    ).astype(jnp.int32)
    micro_pick = (
        micro_index[:, None] == jnp.arange(lengths.shape[1], dtype=jnp.int32)[None, :]
    ).astype(jnp.int32)
    chosen = jnp.sum(
        replica_pick[:, :, None] * micro_pick[:, None, :] * lengths[None, :, :], axis=(1, 2)
    )
    live_rows = (within_index < chosen).astype(jnp.float32)
    row_weight = live_rows * (seq_len / chosen.astype(jnp.float32))
    return (live_rows, row_weight)


def local_stats(logits, teacher):
    row_top = jnp.max(logits, axis=1)
    exp_total = jnp.sum(jnp.exp(logits - row_top[:, None]), axis=1)
    teacher_prob = jnp.exp(teacher)
    cross_sum = jnp.sum(teacher_prob * (teacher - logits), axis=1)
    prob_mass = jnp.sum(teacher_prob, axis=1)
    return (row_top, exp_total, cross_sum, prob_mass, teacher_prob)


def finish_rows(
    logits, teacher_prob, row_top, exp_total, cross_sum, prob_mass, live_rows, row_weight
):
    log_norm = row_top + jnp.log(exp_total)
    divergence = live_rows * (cross_sum + log_norm * prob_mass)
    scaled = jnp.exp(logits - log_norm[:, None]) * prob_mass[:, None] - teacher_prob
    logit_grad = (row_weight[:, None] * scaled).astype(jnp.bfloat16)
    return (divergence, logit_grad)


def body(hidden, head_weight, teacher_logprobs, lengths):
    sections = lax.axis_size("section")
    replicas = lax.axis_size("dp")
    tensor_parts = lax.axis_size("tensor")
    half_width = head_weight.shape[0]
    block_rows = hidden.shape[1]
    tensor_id = lax.axis_index("tensor")
    replica_id = lax.axis_index("dp")
    gathered = lax.all_gather(hidden, ("section", "dp"), axis=0, tiled=True).reshape(
        sections * replicas * block_rows, half_width
    )
    part_rows = sections * replicas * block_rows // tensor_parts
    section_blocks = sections // tensor_parts
    picked = gathered
    logits = lax.psum_scatter(
        jnp.dot(picked, head_weight, preferred_element_type=jnp.float32),
        "tensor",
        scatter_dimension=0,
        tiled=True,
    )
    teacher = (
        teacher_logprobs.reshape(replicas, section_blocks, block_rows, -1)
        .transpose(1, 0, 2, 3)
        .reshape(part_rows, -1)
    )
    grid_shape = (section_blocks, replicas, block_rows)
    section_index = lax.broadcasted_iota(jnp.int32, grid_shape, 0) + tensor_id * section_blocks
    replica = lax.broadcasted_iota(jnp.int32, grid_shape, 1).reshape(-1)
    positions = (
        section_index * block_rows + lax.broadcasted_iota(jnp.int32, grid_shape, 2)
    ).reshape(-1)
    live_rows, row_weight = row_weights(lengths, replica, positions, SEQ_MB)
    row_top, exp_total, cross_sum, prob_mass, teacher_prob = local_stats(logits, teacher)
    global_top = lax.pmax(row_top, ("section", "dp"))
    exp_total, cross_sum, prob_mass = lax.psum(
        (exp_total * jnp.exp(row_top - global_top), cross_sum, prob_mass), ("section", "dp")
    )
    divergence, logit_grad = finish_rows(
        logits, teacher_prob, global_top, exp_total, cross_sum, prob_mass, live_rows, row_weight
    )
    own_rows = lax.dynamic_index_in_dim(
        divergence.reshape(grid_shape), replica_id, 1, keepdims=False
    )
    divergence_out = own_rows.reshape(1, section_blocks * block_rows)
    grad_rows = lax.all_gather(logit_grad, "tensor", axis=0, tiled=True)
    picked = grad_rows
    summed = lax.psum_scatter(
        lax.dot_general(
            picked, head_weight, (((1,), (1,)), ((), ())), preferred_element_type=jnp.float32
        ),
        ("section", "dp"),
        scatter_dimension=0,
        tiled=True,
    )
    hidden_grad = summed.astype(jnp.bfloat16).reshape(1, block_rows, half_width)
    return (hidden_grad, divergence_out)


def solution(mesh):
    placed = (
        P("dp", "section", "tensor"),
        P("tensor", ("section", "dp")),
        P(None, "tensor", ("section", "dp")),
        P(),
    )
    return jax.shard_map(
        body,
        mesh=mesh,
        in_specs=placed,
        out_specs=(P("dp", "section", "tensor"), P("dp", "tensor")),
        check_vma=False,
    )
```

profile of v0, /device:TPU:0, one launch (start us, length us, event | category | flops | bytes accessed | tf_op | source)
XLA Modules:
  0.0 1585.0 jit_solution(1791341485844122555)
XLA Ops:
  7.2 0.7 all-gather.3.cloned.1.call-update
  8.0 120.8 %all-gather.3.cloned.1.call-done = bf16[128,8,1792]{2,1,0:T(8,128)(2,1)} async-done(((bf16[1,8,1792]{2,1,0:T(8,128)(2,1)}), bf16[128,8,1792]{2,1,0:T(8,128)(2,1)}) %all-gather.3.cloned.1.call-update) | async-done | bytes 3670032 | tf_op jit(solution)/shard_map/all_gather | solution.py:53
  128.7 6.5 fusion
  135.3 0.0 all-gather.5.cloned.1.call-start
  135.4 0.1 iota_add_fusion
  135.4 0.1 add.59
  135.5 1.6 fusion.4
  137.1 0.1 reduce_sum.41
  137.2 0.1 eq.38
  137.3 2.5 copy.12
  139.8 0.1 multiply_reduce_fusion
  139.9 8.5 reduce-scatter.3.cloned.1.call-done
  148.4 1.5 reduce_max.9
  149.9 349.8 %pmax.7 = f32[512]{0:T(512)S(1)} all-reduce(f32[512]{0:T(512)S(1)} %reduce_max.9), channel_id=1, replica_groups=mesh['section'=16,'dp'=8,'tensor'=2] {'section','dp'}, use_global_device_ids=true, to_apply=%region_3.4 | all-reduce | flops 512 | bytes 4096 | tf_op jit(solution)/shard_map/pmax | solution.py:78
  499.7 2.5 fusion.3
  502.3 346.4 %all-reduce = (f32[512]{0:T(512)S(1)}, f32[512]{0:T(512)S(1)}, f32[512]{0:T(512)S(1)}) all-reduce(f32[512]{0:T(512)S(1)} %reduce_sum.41, f32[512]{0:T(512)S(1)} %exponential_multiply_fusion, f32[512]{0:T(512)S(1)} %get-tuple-element.2), channel_id=1, replica_groups=mesh['section'=16,'dp'=8,'tensor'=2] {'section','dp'}, use_global_device_ids=true, to_apply=%region_7.8 | all-reduce | flops 1536 | bytes 12288 | tf_op jit(solution)/shard_map/psum | solution.py:79
  848.7 3.0 multiply_convert_fusion
  851.7 0.0 reduce-scatter.5.cloned.1.call-start
  851.8 7.7 all-gather.5.cloned.1.call-done
  859.4 6.7 fusion.10
  866.1 0.1 reshape.129
  866.3 0.6 reshape.130
  866.8 710.2 %reduce-scatter.5.cloned.1.call-done = f32[8,1792]{1,0:T(8,128)} async-done(((f32[1024,1792]{1,0:T(8,128)}), f32[8,1792]{1,0:T(8,128)}) %reduce-scatter.5.cloned.1.call-update) | async-done | bytes 57360 | tf_op jit(solution)/shard_map/reduce_scatter | solution.py:91
  1577.0 1.4 convert_bitcast_fusion
  (18 shorter events, 0.2 us)
Async XLA Ops:
  7.2 121.6 %copy-start = (bf16[1792,640]{1,0:T(8,128)(2,1)S(1)}, bf16[1792,640]{1,0:T(8,128)(2,1)}, u32[]{:S(2)}) copy-start(bf16[1792,640]{1,0:T(8,128)(2,1)} %param.5) | copy-start | bytes 6881284
  7.2 121.5 %all-gather.3.cloned.1.call-start = ((), (), s32[]{:S(2)}) async-start(), calls=%async_computation.2 | async-start | bytes 3698688 | tf_op jit(solution)/shard_map/all_gather | solution.py:53
  7.9 140.5 %reduce-scatter.3.cloned.1.call-start = ((), (), s32[]{:S(2)}) async-start(), calls=%async_computation.3 | async-start | bytes 3932160 | tf_op jit(solution)/shard_map/reduce_scatter | solution.py:59
  135.3 724.2 %all-gather.5.cloned.1.call-start = ((), (), s32[]{:S(2)}) async-start(), calls=%async_computation.4 | async-start | bytes 1966080 | tf_op jit(solution)/shard_map/all_gather | solution.py:89
  137.3 2.5 copy-start.1
  851.7 725.3 %reduce-scatter.5.cloned.1.call-start = ((), (), s32[]{:S(2)}) async-start(), calls=%async_computation.5 | async-start | bytes 7397376 | tf_op jit(solution)/shard_map/reduce_scatter | solution.py:91
Sparse Core Ops, SparseCore 0:
  11.5 117.1 all-gather.2
  135.4 12.9 reduce-scatter.2
  851.8 7.5 all-gather.4
  866.2 710.7 reduce-scatter.4
where the time goes:
time: 1590 us; the launch traced here: 1580 us
  waiting for transfers between devices  848 us (53%)
  blocking collectives  696 us (44%)
    reduce_scatter x1, waiting for transfers between devices, body(): lax.psum_scatter(lax.dot_general(picked, head_weight, (((1,), (1,)), ((),...  710 us
    pmax x1, blocking collectives, body(): global_top = lax.pmax(row_top, ('section', 'dp'))  350 us
    psum x1, blocking collectives, body(): lax.psum((exp_total * jnp.exp(row_top - global_top), cross_sum, prob_mass...  346 us
    all_gather x1, waiting for transfers between devices, body(): lax.all_gather(hidden, ('section', 'dp'), axis=0, tiled=True)  121 us
  transfers between devices with their start and end apart: 4, of which 4 were waited for; matrix products, arithmetic and copies ran while one was open for 0% of the time, Pallas kernels for 0%

commit v1 on v0

v1 whole, which is shorter than its diff:
```python
import jax
import jax.numpy as jnp
from jax import lax
from jax.experimental import pallas as pl
from jax.experimental.pallas import tpu as pltpu
from jax.sharding import PartitionSpec as P

SEQ_MB = 32
NX, NY, NZ = 4, 4, 8
F32, BF16 = jnp.float32, jnp.bfloat16


def kernel(
    hid_ref, w_hbm, tl_hbm, len_ref, grad_ref, div_ref,
    w, tl, tp, zb, hb, lsend, lrecv, lown, stats, rz, ry, rx, g,
    s1, f1, own1, r1h, r1f, tt, s2, r2h, r2f, u, s3, r3,
    lsem, ssem, rsem,
):
    width = w.shape[0]
    half = width // 2
    vocab = w.shape[1]
    section, z, t = lax.axis_index("section"), lax.axis_index("dp"), lax.axis_index("tensor")
    x, y = section // NY, section % NY
    other = 1 - t

    def at_x(k):
        return (((x + k) % NX) * NY + y, z, t)

    def at_y(k):
        return (x * NY + (y + k) % NY, z, t)

    def at_z(k):
        return (section, (z + k) % NZ, t)

    partner = (section, z, other)
    count = [0]

    def send(src, dst, device):
        i = count[0]
        count[0] += 1
        copy = pltpu.make_async_remote_copy(
            src_ref=src, dst_ref=dst, send_sem=ssem.at[i], recv_sem=rsem.at[i],
            device_id=device, device_id_type=pl.DeviceIdType.MESH,
        )
        copy.start()
        started.append(copy)
        return copy

    started = []

    loads = [pltpu.make_async_copy(w_hbm, w, lsem.at[0])]
    for k in range(8):
        loads.append(pltpu.make_async_copy(tl_hbm.at[:, pl.ds(8 * k, 8), :], tl.at[k], lsem.at[k + 1]))
    for load in loads:
        load.start()

    barrier = pltpu.get_barrier_semaphore()
    peers = [at_x(k) for k in range(1, NX)] + [at_y(k) for k in range(1, NY)]
    peers += [at_z(k) for k in range(1, NZ)] + [partner]
    for peer in peers:
        pl.semaphore_signal(barrier, inc=1, device_id=peer, device_id_type=pl.DeviceIdType.MESH)
    pl.semaphore_wait(barrier, len(peers))

    cols = (pl.ds(0, half), pl.ds(half, half))
    copies = [send(hid_ref.at[0], zb.at[z], at_z(k)) for k in (4, 3, 5, 2, 6, 1, 7)]
    zb[z] = hid_ref[0]
    for copy in copies:
        copy.wait_recv()
    hb[x, y] = zb[...].astype(F32).reshape(NZ * 8, width).astype(BF16)

    a_right = send(hb.at[x, y, :, cols[0]], hb.at[x, y, :, cols[0]], at_y(1))
    b_right = send(hb.at[x, y, :, cols[1]], hb.at[x, y, :, cols[1]], at_x(1))
    a_left = send(hb.at[x, y, :, cols[0]], hb.at[x, y, :, cols[0]], at_y(3))
    b_left = send(hb.at[x, y, :, cols[1]], hb.at[x, y, :, cols[1]], at_x(3))
    low, high = pl.ds(0, 32), pl.ds(32, 32)
    y1, y3, x1, x3 = (y + 1) % NY, (y + 3) % NY, (x + 1) % NX, (x + 3) % NX
    a_right.wait_recv()
    c0 = send(hb.at[x, y3, low, cols[0]], hb.at[x, y3, low, cols[0]], at_y(1))
    b_right.wait_recv()
    c1 = send(hb.at[x3, y, low, cols[1]], hb.at[x3, y, low, cols[1]], at_x(1))
    a_left.wait_recv()
    c2 = send(hb.at[x, y1, high, cols[0]], hb.at[x, y1, high, cols[0]], at_y(3))
    b_left.wait_recv()
    c3 = send(hb.at[x1, y, high, cols[1]], hb.at[x1, y, high, cols[1]], at_x(3))
    for copy in (c0, c1, c2, c3):
        copy.wait_recv()

    lo2, hi2 = pl.ds(0, 2), pl.ds(2, 2)

    def a_block(i, part):
        return hb.at[i, part, :, cols[0]]

    def b_block(i, part):
        return hb.at[part, i, :, cols[1]]

    ar0 = send(a_block(x, lo2), a_block(x, lo2), at_x(1))
    br0 = send(b_block(y, lo2), b_block(y, lo2), at_y(1))
    al0 = send(a_block(x, hi2), a_block(x, hi2), at_x(3))
    bl0 = send(b_block(y, hi2), b_block(y, hi2), at_y(3))
    ar1 = send(a_block(x, hi2), a_block(x, hi2), at_x(1))
    br1 = send(b_block(y, hi2), b_block(y, hi2), at_y(1))
    al1 = send(a_block(x, lo2), a_block(x, lo2), at_x(3))
    bl1 = send(b_block(y, lo2), b_block(y, lo2), at_y(3))
    ar0.wait_recv()
    ar2 = send(a_block(x3, lo2), a_block(x3, lo2), at_x(1))
    br0.wait_recv()
    br2 = send(b_block(y3, lo2), b_block(y3, lo2), at_y(1))
    al0.wait_recv()
    al2 = send(a_block(x1, hi2), a_block(x1, hi2), at_x(3))
    bl0.wait_recv()
    bl2 = send(b_block(y1, hi2), b_block(y1, hi2), at_y(3))

    for load in loads:
        load.wait()

    def teacher_block(k, carry):
        tp[k] = jnp.exp(tl[k])
        return carry

    lax.fori_loop(0, 8, teacher_block, 0)

    for copy in (ar1, br1, al1, bl1, ar2, br2, al2, bl2):
        copy.wait_recv()

    exchanges = []
    for j in range(2):
        rows = hb[2 * other + j].reshape(256, width)
        lsend[j] = jnp.dot(rows, w[...], preferred_element_type=F32)
        exchanges.append(send(lsend.at[j], lrecv.at[j], partner))
    for j in range(2):
        rows = hb[2 * t + j].reshape(256, width)
        lown[j] = jnp.dot(rows, w[...], preferred_element_type=F32)

    row_i = lax.broadcasted_iota(jnp.int32, (128, 128), 0)
    lane_i = lax.broadcasted_iota(jnp.int32, (128, 128), 1)
    eye = row_i == lane_i

    def to_lanes(col):
        return jnp.sum(jnp.where(eye, col, 0.0), axis=0, keepdims=True)

    def to_rows(lane):
        return jnp.sum(jnp.where(eye, lane, 0.0), axis=1, keepdims=True)

    for k in range(4):
        j, r = k // 2, (k % 2) * 128
        if k % 2 == 0:
            exchanges[j].wait_recv()
        logits = lown[j, r:r + 128, :] + lrecv[j, r:r + 128, :]
        lown[j, r:r + 128, :] = logits
        teacher = tl[2 * k:2 * k + 2].reshape(128, vocab)
        prob = tp[2 * k:2 * k + 2].reshape(128, vocab)
        top = jnp.max(logits, axis=1, keepdims=True)
        total = jnp.sum(jnp.exp(logits - top), axis=1, keepdims=True)
        cross = jnp.sum(prob * (teacher - logits), axis=1, keepdims=True)
        mass = jnp.sum(prob, axis=1, keepdims=True)
        stats[0, k:k + 1, :] = to_lanes(top)
        stats[0, 4 + k:5 + k, :] = to_lanes(total)
        stats[0, 8 + k:9 + k, :] = to_lanes(cross)
        stats[0, 12 + k:13 + k, :] = to_lanes(mass)

    for level, (slots, at, n) in enumerate(((rz, at_z, NZ), (ry, at_y, NY), (rx, at_x, NX))):
        copies = [send(stats.at[level], slots.at[k - 1], at(k)) for k in range(1, n)]
        for copy in copies:
            copy.wait_recv()
        parts = [stats[level]] + [slots[k] for k in range(n - 1)]
        top = parts[0][0:4]
        for part in parts[1:]:
            top = jnp.maximum(top, part[0:4])
        total = sum(part[4:8] * jnp.exp(part[0:4] - top) for part in parts)
        sums = sum(part[8:16] for part in parts)
        stats[level + 1, 0:4, :] = top
        stats[level + 1, 4:8, :] = total
        stats[level + 1, 8:16, :] = sums

    log_norm = stats[3, 0:4, :] + jnp.log(stats[3, 4:8, :])
    cross, mass = stats[3, 8:12, :], stats[3, 12:16, :]
    row_id = lax.broadcasted_iota(jnp.int32, (4, 128), 0) * 128 + lax.broadcasted_iota(jnp.int32, (4, 128), 1)
    local_section, replica, inner = row_id // 64, (row_id // 8) % 8, row_id % 8
    within = (local_section % 4) * 8 + inner
    micro = local_section // 4
    chosen = jnp.ones((4, 128), jnp.int32)
    for r in range(NZ):
        for m in range(2):
            length = jnp.where(t == 0, len_ref[r, m], len_ref[r, m + 2])
            chosen = jnp.where((replica == r) & (micro == m), length, chosen)
    live = (within < chosen).astype(F32)
    weight = live * (SEQ_MB / chosen.astype(F32))
    divergence = live * (cross + log_norm * mass)
    scale = weight * mass

    div_total = jnp.zeros((1, 128), F32)
    for k in range(4):
        j, r = k // 2, (k % 2) * 128
        norm_rows = to_rows(log_norm[k:k + 1])
        scale_rows = to_rows(scale[k:k + 1])
        weight_rows = to_rows(weight[k:k + 1])
        logits = lown[j, r:r + 128, :]
        prob = tp[2 * k:2 * k + 2].reshape(128, vocab)
        grad = jnp.exp(logits - norm_rows) * scale_rows - weight_rows * prob
        for h in range(2):
            g[2 * t + j, (k % 2) * 2 + h] = grad[64 * h:64 * h + 64].astype(BF16)
        div_rows = to_rows(divergence[k:k + 1])
        place = (2 * k + row_i // 64) * 8 + row_i % 8
        pick = (lane_i == place) & ((row_i // 8) % 8 == z)
        div_total = div_total + jnp.sum(jnp.where(pick, div_rows, 0.0), axis=0, keepdims=True)
    div_ref[...] = div_total[:, 0:64]
    swap = send(g.at[pl.ds(2 * t, 2)], g.at[pl.ds(2 * t, 2)], partner)
    swap.wait_recv()

    def product(part, o):
        if part == 0:
            rows = g[(x + o) % NX]
        else:
            rows = g[:, (y + o) % NY]
        return lax.dot_general(
            rows.reshape(256, vocab), w[pl.ds(part * half, half), :], (((1,), (1,)), ((), ())),
            preferred_element_type=F32,
        ).reshape(4, 64, half)

    first = (at_x, at_y)
    second = (at_y, at_x)
    place2 = (y, x)
    hop, direct = [], []
    for part in range(2):
        s1[part, 2] = product(part, 2).astype(BF16)
        hop.append((
            send(s1.at[part, 2, lo2], r1h.at[part, 0], first[part](1)),
            send(s1.at[part, 2, hi2], r1h.at[part, 1], first[part](3)),
        ))
    for part in range(2):
        block = product(part, 1)
        f1[part, 0] = block[0:2]
        s1[part, 1, 2:4] = block[2:4].astype(BF16)
        direct.append(send(s1.at[part, 1, hi2], r1f.at[part, 0, hi2], first[part](1)))
        block = product(part, 3)
        f1[part, 1] = block[2:4]
        s1[part, 3, 0:2] = block[0:2].astype(BF16)
        direct.append(send(s1.at[part, 3, lo2], r1f.at[part, 1, lo2], first[part](3)))
    for part in range(2):
        hop[part][0].wait_recv()
        s1[part, 1, 0:2] = (f1[part, 0] + r1h[part, 0].astype(F32)).astype(BF16)
        direct.append(send(s1.at[part, 1, lo2], r1f.at[part, 0, lo2], first[part](1)))
        hop[part][1].wait_recv()
        s1[part, 3, 2:4] = (f1[part, 1] + r1h[part, 1].astype(F32)).astype(BF16)
        direct.append(send(s1.at[part, 3, hi2], r1f.at[part, 1, hi2], first[part](3)))
    for part in range(2):
        own1[part] = product(part, 0)
    for copy in direct:
        copy.wait_recv()
    hop, direct = [], []
    for part in range(2):
        def chunk(o):
            i = (place2[part] + o) % 4
            return own1[part, i] + r1f[part, 0, i].astype(F32) + r1f[part, 1, i].astype(F32)

        s2[part, 2] = chunk(2).astype(BF16)
        hop.append((
            send(s2.at[part, 2, low], r2h.at[part, 0], second[part](1)),
            send(s2.at[part, 2, high], r2h.at[part, 1], second[part](3)),
        ))
        tt[part, 1] = chunk(1)
        tt[part, 3] = chunk(3)
        tt[part, 0] = chunk(0)
        s2[part, 1, 32:64] = tt[part, 1, 32:64].astype(BF16)
        direct.append(send(s2.at[part, 1, high], r2f.at[part, 0, high], second[part](1)))
        s2[part, 3, 0:32] = tt[part, 3, 0:32].astype(BF16)
        direct.append(send(s2.at[part, 3, low], r2f.at[part, 1, low], second[part](3)))
    for part in range(2):
        hop[part][0].wait_recv()
        s2[part, 1, 0:32] = (tt[part, 1, 0:32] + r2h[part, 0].astype(F32)).astype(BF16)
        direct.append(send(s2.at[part, 1, low], r2f.at[part, 0, low], second[part](1)))
        hop[part][1].wait_recv()
        s2[part, 3, 32:64] = (tt[part, 3, 32:64] + r2h[part, 1].astype(F32)).astype(BF16)
        direct.append(send(s2.at[part, 3, high], r2f.at[part, 1, high], second[part](3)))
    for copy in direct:
        copy.wait_recv()
    for part in range(2):
        block = tt[part, 0] + r2f[part, 0].astype(F32) + r2f[part, 1].astype(F32)
        u[:, :, part * half:(part + 1) * half] = block.reshape(NZ, 8, half)
    s3[...] = u[...].astype(BF16)
    copies = [send(s3.at[(z + k) % NZ], r3.at[k - 1], at_z(k)) for k in (4, 3, 5, 2, 6, 1, 7)]
    for copy in copies:
        copy.wait_recv()
    total = u[z]
    for k in range(NZ - 1):
        total = total + r3[k].astype(F32)
    grad_ref[0] = total.astype(BF16)

    for copy in started:
        copy.wait_send()


N_SEM = 80


def body(hidden, head_weight, teacher_logprobs, lengths):
    width, vocab = head_weight.shape
    half = width // 2
    V = pltpu.VMEM
    scratch = [
        V((width, vocab), BF16),
        V((8, 8, 8, vocab), F32),
        V((8, 8, 8, vocab), F32),
        V((NZ, 8, width), BF16),
        V((NX, NY, 64, width), BF16),
        V((2, 256, vocab), F32),
        V((2, 256, vocab), F32),
        V((2, 256, vocab), F32),
        V((4, 16, 128), F32),
        V((NZ - 1, 16, 128), F32),
        V((NY - 1, 16, 128), F32),
        V((NX - 1, 16, 128), F32),
        V((NX, NY, 64, vocab), BF16),
        V((2, 4, 4, 64, half), BF16),
        V((2, 2, 2, 64, half), F32),
        V((2, 4, 64, half), F32),
        V((2, 2, 2, 64, half), BF16),
        V((2, 2, 4, 64, half), BF16),
        V((2, 4, 64, half), F32),
        V((2, 4, 64, half), BF16),
        V((2, 2, 32, half), BF16),
        V((2, 2, 64, half), BF16),
        V((NZ, 8, width), F32),
        V((NZ, 8, width), BF16),
        V((NZ - 1, 8, width), BF16),
        pltpu.SemaphoreType.DMA((9,)),
        pltpu.SemaphoreType.DMA((N_SEM,)),
        pltpu.SemaphoreType.DMA((N_SEM,)),
    ]
    return pl.pallas_call(
        kernel,
        out_shape=(
            jax.ShapeDtypeStruct((1, 8, width), BF16),
            jax.ShapeDtypeStruct((1, 64), F32),
        ),
        in_specs=[
            pl.BlockSpec(memory_space=V),
            pl.BlockSpec(memory_space=pl.ANY),
            pl.BlockSpec(memory_space=pl.ANY),
            pl.BlockSpec(memory_space=pltpu.SMEM),
        ],
        out_specs=(pl.BlockSpec(memory_space=V), pl.BlockSpec(memory_space=V)),
        scratch_shapes=scratch,
        compiler_params=pltpu.CompilerParams(
            collective_id=0, has_side_effects=True, vmem_limit_bytes=56 * 1024 * 1024
        ),
        name="distill",
    )(hidden, head_weight, teacher_logprobs, lengths)


def solution(mesh):
    placed = (
        P("dp", "section", "tensor"),
        P("tensor", ("section", "dp")),
        P(None, "tensor", ("section", "dp")),
        P(),
    )
    return jax.shard_map(
        body,
        mesh=mesh,
        in_specs=placed,
        out_specs=(P("dp", "section", "tensor"), P("dp", "tensor")),
        check_vma=False,
    )
```

time: 1590 us -> 98.7 us (0.06)
  the two profiles are of different devices: /device:TPU:0 before, /device:TPU:1 now
where the time goes in v1:
time: 98.7 us; the launch traced here: 98.5 us
  Pallas kernels  94 us (95%)
  local copies, waits for them, and re-layouts  3.88 us (4%)
    pallas_call x1, Pallas kernels, body(): pl.pallas_call(kernel, out_shape=(jax.ShapeDtypeStruct((1, 8, width), BF1...  94 us
    unnamed x3, local copies, waits for them, and re-layouts  3.88 us

profile of v1, /device:TPU:1, one launch (start us, length us, event | category | flops | bytes accessed | tf_op | source)
XLA Modules:
  0.0 98.5 jit_solution(15866601834114244820)
XLA Ops:
  0.6 1.3 %copy.6.len_ref = s32[8,4]{1,0:T(8,128)} copy(s32[8,4]{0,1:T(4,128)} %param.7) | data formatting | bytes 256 | tf_op args[3]
  2.0 94.0 %distill.1 = (bf16[1,8,1792]{2,1,0:T(8,128)(2,1)}, f32[1,64]{1,0:T(1,128)}) custom-call(bf16[1,8,1792]{2,1,0:T(8,128)(2,1)} %hid_ref.1, bf16[1792,640]{1,0:T(8,128)(2,1)} %w_hbm.1, f32[8,64,640]{2,1,0:T(8,128)} %tl_hbm.1, s32[8,4]{1,0:T(8,128)} %copy.6.len_ref), custom_call_target="tpu_custom_call" | custom-call | tf_op jit(solution)/shard_map/distill/pallas_call | solution.py:330
  96.0 1.4 %copy.9 = bf16[1,8,1792]{2,1,0:T(8,128)(2,1)} copy(bf16[1,8,1792]{2,1,0:T(8,128)(2,1)} %get-tuple-element.4) | data formatting | bytes 57344
  97.3 1.2 %copy.10 = f32[1,64]{1,0:T(1,128)} copy(f32[1,64]{1,0:T(1,128)} %get-tuple-element.5) | data formatting | bytes 512

commit v2 on v1

v2 whole, which is shorter than its diff:
```python
import jax
import jax.numpy as jnp
from jax import lax
from jax.experimental import pallas as pl
from jax.experimental.pallas import tpu as pltpu
from jax.sharding import PartitionSpec as P

SEQ_MB = 32
NX, NY, NZ = 4, 4, 8
NA, NB = 512, 768
F32, BF16 = jnp.float32, jnp.bfloat16


def kernel(
    hid_ref, w_hbm, tl_hbm, len_hbm, grad_ref, div_ref,
    w, tl, tp, lengths, zb, pb, hb, bz, lsend, lrecv, lown, stats, rz, rp, g,
    s1, f1, own1, r1h, r1f, s2, r2, u, s3, r3, prod, sb, rb, s4, r4,
    lsem, ssem, rsem,
):
    wide = NA + NA
    vocab = w.shape[1]
    section, z, t = lax.axis_index("section"), lax.axis_index("dp"), lax.axis_index("tensor")
    x, y = section // NY, section % NY
    other = 1 - t

    def at_x(k):
        return (((x + k) % NX) * NY + y, z, t)

    def at_y(k):
        return (x * NY + (y + k) % NY, z, t)

    def at_z(k):
        return (section, (z + k) % NZ, t)

    def plane(k):
        return ((x + k // NY) % NX) * NY + (y + k % NY) % NY

    def at_p(k):
        return (plane(k), z, t)

    far_z = (4, 3, 5, 2, 6, 1, 7)
    far_p = (10, 6, 14, 9, 11, 2, 8, 5, 7, 13, 15, 1, 3, 4, 12)
    partner = (section, z, other)
    started = []

    def send(src, dst, device):
        i = len(started)
        copy = pltpu.make_async_remote_copy(
            src_ref=src, dst_ref=dst, send_sem=ssem.at[i], recv_sem=rsem.at[i],
            device_id=device, device_id_type=pl.DeviceIdType.MESH,
        )
        copy.start()
        started.append(copy)
        return copy

    barrier = pltpu.get_barrier_semaphore()
    peers = [at_z(k) for k in far_z] + [at_p(k) for k in far_p] + [partner]
    for peer in peers:
        pl.semaphore_signal(barrier, inc=1, device_id=peer, device_id_type=pl.DeviceIdType.MESH)

    loads = [pltpu.make_async_copy(w_hbm, w, lsem.at[0]), pltpu.make_async_copy(len_hbm, lengths, lsem.at[9])]
    for k in range(8):
        loads.append(pltpu.make_async_copy(tl_hbm.at[:, pl.ds(8 * k, 8), :], tl.at[k], lsem.at[k + 1]))
    for load in loads:
        load.start()
    pl.semaphore_wait(barrier, len(peers))

    ca, cc, cac, cb = pl.ds(0, NA), pl.ds(NA, NA), pl.ds(0, wide), pl.ds(wide, NB)
    zs = [send(hid_ref.at[0, :, cac], zb.at[z], at_z(k)) for k in far_z]
    ps = [send(hid_ref.at[0, :, cb], pb.at[section], at_p(k)) for k in far_p]
    zb[z] = hid_ref[0, :, 0:wide]
    pb[section] = hid_ref[0, :, wide:]
    for copy in zs:
        copy.wait_recv()
    hb[x, y] = zb[...].astype(F32).reshape(NZ * 8, wide).astype(BF16)
    ph2 = []
    for k in (2, 1, 3):
        ph2.append(send(hb.at[x, y, :, ca], hb.at[x, y, :, ca], at_y(k)))
        ph2.append(send(hb.at[x, y, :, cc], hb.at[x, y, :, cc], at_x(k)))
    for copy in ps:
        copy.wait_recv()
    bz[z] = pb[...].astype(F32).reshape(128, NB).astype(BF16)

    top_half, low_half = pl.ds(0, 64), pl.ds(64, 64)

    def b_pass(step, right, rows):
        block = bz.at[(z - step) % NZ if right else (z + step) % NZ, rows]
        return send(block, block, at_z(1 if right else NZ - 1))

    ring = [[b_pass(0, True, top_half), b_pass(0, False, low_half), b_pass(0, True, low_half), b_pass(0, False, top_half)]]

    def b_forward(step, which):
        ring[step - 1][which].wait_recv()
        right = which in (0, 2)
        ring[step].append(b_pass(step, right, top_half if which in (0, 3) else low_half))

    ring.append([])
    for which in range(4):
        b_forward(1, which)

    for copy in ph2:
        copy.wait_recv()
    y1, y3, x1, x3 = (y + 1) % NY, (y + 3) % NY, (x + 1) % NX, (x + 3) % NX
    lo2, hi2 = pl.ds(0, 2), pl.ds(2, 2)

    def a_block(i, part):
        return hb.at[i, part, :, ca]

    def c_block(i, part):
        return hb.at[part, i, :, cc]

    ar0 = send(a_block(x, lo2), a_block(x, lo2), at_x(1))
    br0 = send(c_block(y, lo2), c_block(y, lo2), at_y(1))
    al0 = send(a_block(x, hi2), a_block(x, hi2), at_x(3))
    bl0 = send(c_block(y, hi2), c_block(y, hi2), at_y(3))
    ar1 = send(a_block(x, hi2), a_block(x, hi2), at_x(1))
    br1 = send(c_block(y, hi2), c_block(y, hi2), at_y(1))
    al1 = send(a_block(x, lo2), a_block(x, lo2), at_x(3))
    bl1 = send(c_block(y, lo2), c_block(y, lo2), at_y(3))

    for load in loads:
        load.wait()

    def teacher_block(k, carry):
        tp[k] = jnp.exp(tl[k])
        return carry

    lax.fori_loop(0, 8, teacher_block, 0)

    ring.append([])
    for which in range(4):
        b_forward(2, which)
    ar0.wait_recv()
    ar2 = send(a_block(x3, lo2), a_block(x3, lo2), at_x(1))
    br0.wait_recv()
    br2 = send(c_block(y3, lo2), c_block(y3, lo2), at_y(1))
    al0.wait_recv()
    al2 = send(a_block(x1, hi2), a_block(x1, hi2), at_x(3))
    bl0.wait_recv()
    bl2 = send(c_block(y1, hi2), c_block(y1, hi2), at_y(3))
    ring.append([])
    for which in range(2):
        b_forward(3, which)
    for copy in [ar1, br1, al1, bl1] + ring[2][2:4] + [ar2, br2, al2, bl2] + ring[3]:
        copy.wait_recv()

    w_top, w_low = w[0:wide], w[wide:]

    def b_logits(owner, h):
        rows = pl.ds(64 * owner + 32 * h, 32)
        return jnp.dot(bz[:, rows, :].reshape(256, NB), w_low, preferred_element_type=F32).reshape(8, 4, 8, vocab)

    exchanges = []
    for owner, into in ((other, lsend), (t, lown)):
        for h in range(2):
            rows = hb[2 * owner + h].reshape(256, wide)
            block = jnp.dot(rows, w_top, preferred_element_type=F32).reshape(4, 8, 8, vocab)
            extra = b_logits(owner, h)
            for r in range(NZ):
                into[4 * h:4 * h + 4, r] = block[:, r] + extra[r]
            if into is lsend:
                exchanges.append(send(lsend.at[pl.ds(4 * h, 4)], lrecv.at[pl.ds(4 * h, 4)], partner))

    row_i = lax.broadcasted_iota(jnp.int32, (128, 128), 0)
    lane_i = lax.broadcasted_iota(jnp.int32, (128, 128), 1)
    eye = row_i == lane_i

    def to_lanes(col):
        return jnp.sum(jnp.where(eye, col, 0.0), axis=0, keepdims=True)

    def to_rows(lane):
        return jnp.sum(jnp.where(eye, lane, 0.0), axis=1, keepdims=True)

    for k in range(4):
        if k % 2 == 0:
            exchanges[k // 2].wait_recv()
        pair = slice(2 * k, 2 * k + 2)
        both = lown[pair] + lrecv[pair]
        lown[pair] = both
        logits = both.reshape(128, vocab)
        teacher = tl[pair].reshape(128, vocab)
        prob = tp[pair].reshape(128, vocab)
        top = jnp.max(logits, axis=1, keepdims=True)
        total = jnp.sum(jnp.exp(logits - top), axis=1, keepdims=True)
        cross = jnp.sum(prob * (teacher - logits), axis=1, keepdims=True)
        mass = jnp.sum(prob, axis=1, keepdims=True)
        stats[0, k:k + 1, :] = to_lanes(top)
        stats[0, 4 + k:5 + k, :] = to_lanes(total)
        stats[0, 8 + k:9 + k, :] = to_lanes(cross)
        stats[0, 12 + k:13 + k, :] = to_lanes(mass)

    for level, (slots, at, order) in enumerate(((rz, at_z, far_z), (rp, at_p, far_p))):
        copies = [send(stats.at[level], slots.at[k - 1], at(k)) for k in order]
        for copy in copies:
            copy.wait_recv()
        parts = [stats[level]] + [slots[k] for k in range(len(order))]
        top = parts[0][0:4]
        for part in parts[1:]:
            top = jnp.maximum(top, part[0:4])
        total = sum(part[4:8] * jnp.exp(part[0:4] - top) for part in parts)
        sums = sum(part[8:16] for part in parts)
        stats[level + 1, 0:4, :] = top
        stats[level + 1, 4:8, :] = total
        stats[level + 1, 8:16, :] = sums

    log_norm = stats[2, 0:4, :] + jnp.log(stats[2, 4:8, :])
    cross, mass = stats[2, 8:12, :], stats[2, 12:16, :]
    row_id = lax.broadcasted_iota(jnp.int32, (4, 128), 0) * 128 + lax.broadcasted_iota(jnp.int32, (4, 128), 1)
    local_section, replica, inner = row_id // 64, (row_id // 8) % 8, row_id % 8
    within = (local_section % 4) * 8 + inner
    micro = local_section // 4
    chosen = jnp.ones((4, 128), jnp.int32)
    for r in range(NZ):
        for m in range(2):
            length = jnp.where(t == 0, lengths[r, m], lengths[r, m + 2])
            chosen = jnp.where((replica == r) & (micro == m), length, chosen)
    live = (within < chosen).astype(F32)
    weight = live * (SEQ_MB / chosen.astype(F32))
    divergence = live * (cross + log_norm * mass)
    scale = weight * mass

    div_total = jnp.zeros((1, 128), F32)
    swaps = []
    for k in range(4):
        norm_rows = to_rows(log_norm[k:k + 1])
        scale_rows = to_rows(scale[k:k + 1])
        weight_rows = to_rows(weight[k:k + 1])
        pair = slice(2 * k, 2 * k + 2)
        logits = lown[pair].reshape(128, vocab)
        prob = tp[pair].reshape(128, vocab)
        grad = jnp.exp(logits - norm_rows) * scale_rows - weight_rows * prob
        g[2 * t + k // 2, 2 * (k % 2):2 * (k % 2) + 2] = grad.astype(BF16).reshape(2, 64, vocab)
        mine = g.at[2 * t + k // 2, pl.ds(2 * (k % 2), 2)]
        swaps.append(send(mine, mine, partner))
    for k in range(4):
        div_rows = to_rows(divergence[k:k + 1])
        place = (2 * k + row_i // 64) * 8 + row_i % 8
        pick = (lane_i == place) & ((row_i // 8) % 8 == z)
        div_total = div_total + jnp.sum(jnp.where(pick, div_rows, 0.0), axis=0, keepdims=True)
    div_ref[...] = div_total[:, 0:64]
    for copy in swaps:
        copy.wait_recv()

    def times_w(rows, start, size):
        return lax.dot_general(
            rows, w[start:start + size, :], (((1,), (1,)), ((), ())), preferred_element_type=F32
        )

    def product(part, o):
        rows = g[(x + o) % NX] if part == 0 else g[:, (y + o) % NY]
        return times_w(rows.reshape(256, vocab), part * NA, NA).reshape(4, 64, NA)

    first = (at_x, at_y)
    second = (at_y, at_x)
    hop, direct = [], []
    for part in range(2):
        s1[part, 2] = product(part, 2).astype(BF16)
        hop.append((
            send(s1.at[part, 2, lo2], r1h.at[part, 0], first[part](1)),
            send(s1.at[part, 2, hi2], r1h.at[part, 1], first[part](3)),
        ))
    for i in range(NX):
        block = times_w(g[i].reshape(256, vocab), wide, NB).reshape(4, 8, 8, NB)
        for r in range(NZ):
            prod[r, 32 * i:32 * i + 32] = block[:, r].reshape(32, NB)

    halves = (slice(0, 64), slice(64, 128))

    def b_item(side, item, extra=None):
        step = 0 if item == 0 else (item + 1) // 2
        upper = (item % 2 == 0) if side == 0 else (item % 2 == 1)
        owner = (z + 4 - step) % NZ if side == 0 else (z + 4 + step) % NZ
        value = prod[owner, halves[0 if upper else 1]]
        if extra is not None:
            value = value + extra
        sb[side, item] = value.astype(BF16)
        return send(sb.at[side, item], rb.at[side, item], at_z(1 if side == 0 else NZ - 1))

    sides = [[b_item(side, 0)] for side in range(2)]
    for side in range(2):
        sides[side].append(b_item(side, 1))

    def b_next(item):
        source = 0 if item == 2 else item - 2
        for side in range(2):
            sides[side][source].wait_recv()
            sides[side].append(b_item(side, item, rb[side, source].astype(F32)))

    for part in range(2):
        block = product(part, 1)
        f1[part, 0] = block[0:2]
        s1[part, 1, 2:4] = block[2:4].astype(BF16)
        direct.append(send(s1.at[part, 1, hi2], r1f.at[part, 0, hi2], first[part](1)))
        block = product(part, 3)
        f1[part, 1] = block[2:4]
        s1[part, 3, 0:2] = block[0:2].astype(BF16)
        direct.append(send(s1.at[part, 3, lo2], r1f.at[part, 1, lo2], first[part](3)))
    for part in range(2):
        own1[part] = product(part, 0)
    for part in range(2):
        hop[part][0].wait_recv()
        s1[part, 1, 0:2] = (f1[part, 0] + r1h[part, 0].astype(F32)).astype(BF16)
        direct.append(send(s1.at[part, 1, lo2], r1f.at[part, 0, lo2], first[part](1)))
        hop[part][1].wait_recv()
        s1[part, 3, 2:4] = (f1[part, 1] + r1h[part, 1].astype(F32)).astype(BF16)
        direct.append(send(s1.at[part, 3, hi2], r1f.at[part, 1, hi2], first[part](3)))
    b_next(2)
    b_next(3)
    b_next(4)
    for copy in direct:
        copy.wait_recv()
    place2 = (y, x)
    ph2 = []
    for k in (2, 1, 3):
        for part in range(2):
            i = (place2[part] + k) % 4
            value = own1[part, i] + r1f[part, 0, i].astype(F32) + r1f[part, 1, i].astype(F32)
            s2[part, k - 1] = value.astype(BF16)
            ph2.append(send(s2.at[part, k - 1], r2.at[part, k - 1], second[part](k)))
    b_next(5)
    b_next(6)
    for copy in ph2:
        copy.wait_recv()
    for part in range(2):
        i = place2[part]
        value = own1[part, i] + r1f[part, 0, i].astype(F32) + r1f[part, 1, i].astype(F32)
        for k in range(3):
            value = value + r2[part, k].astype(F32)
        u[:, :, part * NA:(part + 1) * NA] = value.reshape(NZ, 8, NA)
    s3[...] = u[...].astype(BF16)
    zs = [send(s3.at[(z + k) % NZ], r3.at[k - 1], at_z(k)) for k in far_z]
    for side in range(2):
        for item in (5, 6):
            sides[side][item].wait_recv()
    prod[z, halves[0]] = prod[z, halves[0]] + rb[0, 6].astype(F32) + rb[1, 5].astype(F32)
    prod[z, halves[1]] = prod[z, halves[1]] + rb[0, 5].astype(F32) + rb[1, 6].astype(F32)
    s4[...] = prod[z].reshape(16, 8, NB).astype(BF16)
    ps = [send(s4.at[plane(k)], r4.at[k - 1], at_p(k)) for k in far_p]
    for copy in zs:
        copy.wait_recv()
    total = u[z]
    for k in range(NZ - 1):
        total = total + r3[k].astype(F32)
    grad_ref[0, :, 0:wide] = total.astype(BF16)
    for copy in ps:
        copy.wait_recv()
    total = prod[z, pl.ds(pl.multiple_of(8 * section, 8), 8)]
    for k in range(15):
        total = total + r4[k].astype(F32)
    grad_ref[0, :, wide:] = total.astype(BF16)

    for copy in started:
        copy.wait_send()


N_SEM = 160


def body(hidden, head_weight, teacher_logprobs, lengths):
    width, vocab = head_weight.shape
    wide = 2 * NA
    V = pltpu.VMEM
    scratch = [
        V((width, vocab), BF16),
        V((8, 8, 8, vocab), F32),
        V((8, 8, 8, vocab), F32),
        pltpu.SMEM((8, 4), jnp.int32),
        V((NZ, 8, wide), BF16),
        V((16, 8, NB), BF16),
        V((NX, NY, 64, wide), BF16),
        V((NZ, 128, NB), BF16),
        V((8, 8, 8, vocab), F32),
        V((8, 8, 8, vocab), F32),
        V((8, 8, 8, vocab), F32),
        V((3, 16, 128), F32),
        V((NZ - 1, 16, 128), F32),
        V((15, 16, 128), F32),
        V((NX, NY, 64, vocab), BF16),
        V((2, 4, 4, 64, NA), BF16),
        V((2, 2, 2, 64, NA), F32),
        V((2, 4, 64, NA), F32),
        V((2, 2, 2, 64, NA), BF16),
        V((2, 2, 4, 64, NA), BF16),
        V((2, 3, 64, NA), BF16),
        V((2, 3, 64, NA), BF16),
        V((NZ, 8, wide), F32),
        V((NZ, 8, wide), BF16),
        V((NZ - 1, 8, wide), BF16),
        V((NZ, 128, NB), F32),
        V((2, 7, 64, NB), BF16),
        V((2, 7, 64, NB), BF16),
        V((16, 8, NB), BF16),
        V((15, 8, NB), BF16),
        pltpu.SemaphoreType.DMA((10,)),
        pltpu.SemaphoreType.DMA((N_SEM,)),
        pltpu.SemaphoreType.DMA((N_SEM,)),
    ]
    return pl.pallas_call(
        kernel,
        out_shape=(
            jax.ShapeDtypeStruct((1, 8, width), BF16),
            jax.ShapeDtypeStruct((1, 64), F32),
        ),
        in_specs=[
            pl.BlockSpec(memory_space=V),
            pl.BlockSpec(memory_space=pl.ANY),
            pl.BlockSpec(memory_space=pl.ANY),
            pl.BlockSpec(memory_space=pl.ANY),
        ],
        out_specs=(pl.BlockSpec(memory_space=V), pl.BlockSpec(memory_space=V)),
        scratch_shapes=scratch,
        compiler_params=pltpu.CompilerParams(
            collective_id=0, has_side_effects=True, vmem_limit_bytes=56 * 1024 * 1024
        ),
        name="distill",
    )(hidden, head_weight, teacher_logprobs, lengths)


def solution(mesh):
    placed = (
        P("dp", "section", "tensor"),
        P("tensor", ("section", "dp")),
        P(None, "tensor", ("section", "dp")),
        P(),
    )
    return jax.shard_map(
        body,
        mesh=mesh,
        in_specs=placed,
        out_specs=(P("dp", "section", "tensor"), P("dp", "tensor")),
        check_vma=False,
    )
```

time: 98.7 us -> 82.3 us (0.83)
  Pallas kernels: 94 us -> 77.6 us
    pallas_call x1, Pallas kernels: 94 us -> 77.6 us  [body(): pl.pallas_call(kernel, out_shape=(jax.ShapeDtypeStruct((1, 8, width), BF1...]
where the time goes in v2:
time: 82.3 us; the launch traced here: 82.1 us
  Pallas kernels  77.6 us (94%)
  local copies, waits for them, and re-layouts  3.88 us (5%)
    pallas_call x1, Pallas kernels, body(): pl.pallas_call(kernel, out_shape=(jax.ShapeDtypeStruct((1, 8, width), BF1...  77.6 us
    unnamed x3, local copies, waits for them, and re-layouts  3.88 us

profile of v2, /device:TPU:1, one launch (start us, length us, event | category | flops | bytes accessed | tf_op | source)
XLA Modules:
  0.0 82.1 jit_solution(16863467941164503077)
XLA Ops:
  0.6 1.3 %copy.6.len_hbm = s32[8,4]{1,0:T(8,128)} copy(s32[8,4]{0,1:T(4,128)} %param.7) | data formatting | bytes 256 | tf_op args[3]
  2.0 77.6 %distill.1 = (bf16[1,8,1792]{2,1,0:T(8,128)(2,1)}, f32[1,64]{1,0:T(1,128)}) custom-call(bf16[1,8,1792]{2,1,0:T(8,128)(2,1)} %hid_ref.1, bf16[1792,640]{1,0:T(8,128)(2,1)} %w_hbm.1, f32[8,64,640]{2,1,0:T(8,128)} %tl_hbm.1, s32[8,4]{1,0:T(8,128)} %copy.6.len_hbm), custom_call_target="tpu_custom_call" | custom-call | tf_op jit(solution)/shard_map/distill/pallas_call | solution.py:398
  79.6 1.4 %copy.9 = bf16[1,8,1792]{2,1,0:T(8,128)(2,1)} copy(bf16[1,8,1792]{2,1,0:T(8,128)(2,1)} %get-tuple-element.4) | data formatting | bytes 57344
  80.9 1.2 %copy.10 = f32[1,64]{1,0:T(1,128)} copy(f32[1,64]{1,0:T(1,128)} %get-tuple-element.5) | data formatting | bytes 512

commit v3 on v2

--- a/solution.py
+++ b/solution.py
@@ -12,8 +12,8 @@
 
 
 def kernel(
-    hid_ref, w_hbm, tl_hbm, len_hbm, grad_ref, div_ref,
-    w, tl, tp, lengths, zb, pb, hb, bz, lsend, lrecv, lown, stats, rz, rp, g,
+    hid_hbm, w_hbm, tl_hbm, len_hbm, grad_ref, div_ref,
+    w, tl, tp, lengths, zb, pb, hb, bz, acc, lrecv, stats, rz, rp, g,
     s1, f1, own1, r1h, r1f, s2, r2, u, s3, r3, prod, sb, rb, s4, r4,
     lsem, ssem, rsem,
 ):
@@ -58,18 +58,26 @@
     for peer in peers:
         pl.semaphore_signal(barrier, inc=1, device_id=peer, device_id_type=pl.DeviceIdType.MESH)
 
+    ca, cc, cac, cb = pl.ds(0, NA), pl.ds(NA, NA), pl.ds(0, wide), pl.ds(wide, NB)
+    own_rows = (
+        pltpu.make_async_copy(hid_hbm.at[0, :, cac], zb.at[z], lsem.at[10]),
+        pltpu.make_async_copy(hid_hbm.at[0, :, cb], pb.at[section], lsem.at[11]),
+    )
+    for load in own_rows:
+        load.start()
+
     loads = [pltpu.make_async_copy(w_hbm, w, lsem.at[0]), pltpu.make_async_copy(len_hbm, lengths, lsem.at[9])]
     for k in range(8):
         loads.append(pltpu.make_async_copy(tl_hbm.at[:, pl.ds(8 * k, 8), :], tl.at[k], lsem.at[k + 1]))
     for load in loads:
         load.start()
+    for load in own_rows:
+        load.wait()
     pl.semaphore_wait(barrier, len(peers))
 
-    ca, cc, cac, cb = pl.ds(0, NA), pl.ds(NA, NA), pl.ds(0, wide), pl.ds(wide, NB)
-    zs = [send(hid_ref.at[0, :, cac], zb.at[z], at_z(k)) for k in far_z]
-    ps = [send(hid_ref.at[0, :, cb], pb.at[section], at_p(k)) for k in far_p]
-    zb[z] = hid_ref[0, :, 0:wide]
-    pb[section] = hid_ref[0, :, wide:]
+    zs = [send(zb.at[z], zb.at[z], at_z(k)) for k in far_z]
+    ps = [send(pb.at[section], pb.at[section], at_p(k)) for k in far_p]
+    acc[...] = jnp.zeros_like(acc)
     for copy in zs:
         copy.wait_recv()
     hb[x, y] = zb[...].astype(F32).reshape(NZ * 8, wide).astype(BF16)
@@ -118,6 +126,20 @@
     al1 = send(a_block(x, lo2), a_block(x, lo2), at_x(3))
     bl1 = send(c_block(y, lo2), c_block(y, lo2), at_y(3))
 
+    def a_logits(i):
+        rows = hb[i, :, :, 0:NA].reshape(256, NA)
+        block = jnp.dot(rows, w[0:NA], preferred_element_type=F32)
+        acc[i] = acc[i] + block.reshape(4, 8, 8, vocab)
+
+    def c_logits(i):
+        rows = hb[:, i, :, NA:wide].reshape(256, NA)
+        block = jnp.dot(rows, w[NA:wide], preferred_element_type=F32)
+        acc[:, i] = acc[:, i] + block.reshape(4, 8, 8, vocab)
+
+    def b_logits(i):
+        block = jnp.dot(bz[i], w[wide:], preferred_element_type=F32)
+        acc[:, :, i] = acc[:, :, i] + block.reshape(4, 4, 8, vocab)
+
     for load in loads:
         load.wait()
 
@@ -126,10 +148,15 @@
         return carry
 
     lax.fori_loop(0, 8, teacher_block, 0)
+    b_logits(z)
+    a_logits(x)
+    c_logits(y)
 
     ring.append([])
     for which in range(4):
         b_forward(2, which)
+    b_logits((z + 1) % NZ)
+    b_logits((z + 7) % NZ)
     ar0.wait_recv()
     ar2 = send(a_block(x3, lo2), a_block(x3, lo2), at_x(1))
     br0.wait_recv()
@@ -141,25 +168,30 @@
     ring.append([])
     for which in range(2):
         b_forward(3, which)
-    for copy in [ar1, br1, al1, bl1] + ring[2][2:4] + [ar2, br2, al2, bl2] + ring[3]:
-        copy.wait_recv()
-
-    w_top, w_low = w[0:wide], w[wide:]
-
-    def b_logits(owner, h):
-        rows = pl.ds(64 * owner + 32 * h, 32)
-        return jnp.dot(bz[:, rows, :].reshape(256, NB), w_low, preferred_element_type=F32).reshape(8, 4, 8, vocab)
-
+    b_logits((z + 2) % NZ)
+    b_logits((z + 6) % NZ)
+    for copy in [ar1, br1, al1, bl1]:
+        copy.wait_recv()
+    for k in (1, 3):
+        a_logits((x + k) % NX)
+        c_logits((y + k) % NY)
+    for copy in ring[2][2:4]:
+        copy.wait_recv()
+    b_logits((z + 3) % NZ)
+    b_logits((z + 5) % NZ)
+    for copy in (ar2, al2):
+        copy.wait_recv()
+    a_logits((x + 2) % NX)
+    for copy in (br2, bl2):
+        copy.wait_recv()
+    c_logits((y + 2) % NY)
+    for copy in ring[3]:
+        copy.wait_recv()
+    b_logits((z + 4) % NZ)
     exchanges = []
-    for owner, into in ((other, lsend), (t, lown)):
-        for h in range(2):
-            rows = hb[2 * owner + h].reshape(256, wide)
-            block = jnp.dot(rows, w_top, preferred_element_type=F32).reshape(4, 8, 8, vocab)
-            extra = b_logits(owner, h)
-            for r in range(NZ):
-                into[4 * h:4 * h + 4, r] = block[:, r] + extra[r]
-            if into is lsend:
-                exchanges.append(send(lsend.at[pl.ds(4 * h, 4)], lrecv.at[pl.ds(4 * h, 4)], partner))
+    for k in range(4):
+        block = acc.at[2 * other + k // 2, pl.ds(2 * (k % 2), 2)]
+        exchanges.append(send(block, lrecv.at[pl.ds(2 * k, 2)], partner))
 
     row_i = lax.broadcasted_iota(jnp.int32, (128, 128), 0)
     lane_i = lax.broadcasted_iota(jnp.int32, (128, 128), 1)
@@ -172,11 +204,10 @@
         return jnp.sum(jnp.where(eye, lane, 0.0), axis=1, keepdims=True)
 
     for k in range(4):
-        if k % 2 == 0:
-            exchanges[k // 2].wait_recv()
+        exchanges[k].wait_recv()
         pair = slice(2 * k, 2 * k + 2)
-        both = lown[pair] + lrecv[pair]
-        lown[pair] = both
+        both = acc[2 * t + k // 2, 2 * (k % 2):2 * (k % 2) + 2] + lrecv[pair]
+        lrecv[pair] = both
         logits = both.reshape(128, vocab)
         teacher = tl[pair].reshape(128, vocab)
         prob = tp[pair].reshape(128, vocab)
@@ -212,7 +243,7 @@
     chosen = jnp.ones((4, 128), jnp.int32)
     for r in range(NZ):
         for m in range(2):
-            length = jnp.where(t == 0, lengths[r, m], lengths[r, m + 2])
+            length = jnp.where(t == 0, lengths[m, r], lengths[m + 2, r])
             chosen = jnp.where((replica == r) & (micro == m), length, chosen)
     live = (within < chosen).astype(F32)
     weight = live * (SEQ_MB / chosen.astype(F32))
@@ -226,10 +257,10 @@
         scale_rows = to_rows(scale[k:k + 1])
         weight_rows = to_rows(weight[k:k + 1])
         pair = slice(2 * k, 2 * k + 2)
-        logits = lown[pair].reshape(128, vocab)
+        logits = lrecv[pair].reshape(128, vocab)
         prob = tp[pair].reshape(128, vocab)
         grad = jnp.exp(logits - norm_rows) * scale_rows - weight_rows * prob
-        g[2 * t + k // 2, 2 * (k % 2):2 * (k % 2) + 2] = grad.astype(BF16).reshape(2, 64, vocab)
+        g[2 * t + k // 2, 2 * (k % 2):2 * (k % 2) + 2] = grad.reshape(2, 8, 8, vocab).astype(BF16)
         mine = g.at[2 * t + k // 2, pl.ds(2 * (k % 2), 2)]
         swaps.append(send(mine, mine, partner))
     for k in range(4):
@@ -248,22 +279,16 @@
 
     def product(part, o):
         rows = g[(x + o) % NX] if part == 0 else g[:, (y + o) % NY]
-        return times_w(rows.reshape(256, vocab), part * NA, NA).reshape(4, 64, NA)
+        rows = rows.astype(F32).reshape(256, vocab).astype(BF16)
+        return times_w(rows, part * NA, NA).reshape(4, 64, NA)
+
+    def b_product(o):
+        i = (z + o) % NZ
+        rows = g[:, :, i].astype(F32).reshape(128, vocab).astype(BF16)
+        prod[i] = times_w(rows, wide, NB)
 
     first = (at_x, at_y)
     second = (at_y, at_x)
-    hop, direct = [], []
-    for part in range(2):
-        s1[part, 2] = product(part, 2).astype(BF16)
-        hop.append((
-            send(s1.at[part, 2, lo2], r1h.at[part, 0], first[part](1)),
-            send(s1.at[part, 2, hi2], r1h.at[part, 1], first[part](3)),
-        ))
-    for i in range(NX):
-        block = times_w(g[i].reshape(256, vocab), wide, NB).reshape(4, 8, 8, NB)
-        for r in range(NZ):
-            prod[r, 32 * i:32 * i + 32] = block[:, r].reshape(32, NB)
-
     halves = (slice(0, 64), slice(64, 128))
 
     def b_item(side, item, extra=None):
@@ -276,8 +301,17 @@
         sb[side, item] = value.astype(BF16)
         return send(sb.at[side, item], rb.at[side, item], at_z(1 if side == 0 else NZ - 1))
 
+    hop, direct = [], []
+    b_product(4)
     sides = [[b_item(side, 0)] for side in range(2)]
+    for part in range(2):
+        s1[part, 2] = product(part, 2).astype(BF16)
+        hop.append((
+            send(s1.at[part, 2, lo2], r1h.at[part, 0], first[part](1)),
+            send(s1.at[part, 2, hi2], r1h.at[part, 1], first[part](3)),
+        ))
     for side in range(2):
+        b_product((3, 5)[side])
         sides[side].append(b_item(side, 1))
 
     def b_next(item):
@@ -295,8 +329,9 @@
         f1[part, 1] = block[2:4]
         s1[part, 3, 0:2] = block[0:2].astype(BF16)
         direct.append(send(s1.at[part, 3, lo2], r1f.at[part, 1, lo2], first[part](3)))
-    for part in range(2):
-        own1[part] = product(part, 0)
+    b_next(2)
+    b_product(2)
+    b_product(6)
     for part in range(2):
         hop[part][0].wait_recv()
         s1[part, 1, 0:2] = (f1[part, 0] + r1h[part, 0].astype(F32)).astype(BF16)
@@ -304,9 +339,14 @@
         hop[part][1].wait_recv()
         s1[part, 3, 2:4] = (f1[part, 1] + r1h[part, 1].astype(F32)).astype(BF16)
         direct.append(send(s1.at[part, 3, hi2], r1f.at[part, 1, hi2], first[part](3)))
-    b_next(2)
     b_next(3)
+    b_product(1)
+    b_product(7)
+    b_product(0)
+    for part in range(2):
+        own1[part] = product(part, 0)
     b_next(4)
+    b_next(5)
     for copy in direct:
         copy.wait_recv()
     place2 = (y, x)
@@ -317,7 +357,6 @@
             value = own1[part, i] + r1f[part, 0, i].astype(F32) + r1f[part, 1, i].astype(F32)
             s2[part, k - 1] = value.astype(BF16)
             ph2.append(send(s2.at[part, k - 1], r2.at[part, k - 1], second[part](k)))
-    b_next(5)
     b_next(6)
     for copy in ph2:
         copy.wait_recv()
@@ -353,6 +392,11 @@
         copy.wait_send()
 
 
+def hand_over(grad_ref, div_ref, grad_out, div_out):
+    grad_out[...] = grad_ref[...]
+    div_out[...] = div_ref[...]
+
+
 N_SEM = 160
 
 
@@ -364,18 +408,17 @@
         V((width, vocab), BF16),
         V((8, 8, 8, vocab), F32),
         V((8, 8, 8, vocab), F32),
-        pltpu.SMEM((8, 4), jnp.int32),
+        pltpu.SMEM((4, 8), jnp.int32),
         V((NZ, 8, wide), BF16),
         V((16, 8, NB), BF16),
         V((NX, NY, 64, wide), BF16),
         V((NZ, 128, NB), BF16),
-        V((8, 8, 8, vocab), F32),
-        V((8, 8, 8, vocab), F32),
+        V((NX, NY, 8, 8, vocab), F32),
         V((8, 8, 8, vocab), F32),
         V((3, 16, 128), F32),
         V((NZ - 1, 16, 128), F32),
         V((15, 16, 128), F32),
-        V((NX, NY, 64, vocab), BF16),
+        V((NX, NY, 8, 8, vocab), BF16),
         V((2, 4, 4, 64, NA), BF16),
         V((2, 2, 2, 64, NA), F32),
         V((2, 4, 64, NA), F32),
@@ -391,18 +434,18 @@
         V((2, 7, 64, NB), BF16),
         V((16, 8, NB), BF16),
         V((15, 8, NB), BF16),
-        pltpu.SemaphoreType.DMA((10,)),
+        pltpu.SemaphoreType.DMA((12,)),
         pltpu.SemaphoreType.DMA((N_SEM,)),
         pltpu.SemaphoreType.DMA((N_SEM,)),
     ]
-    return pl.pallas_call(
+    grad, divergence = pl.pallas_call(
         kernel,
         out_shape=(
             jax.ShapeDtypeStruct((1, 8, width), BF16),
             jax.ShapeDtypeStruct((1, 64), F32),
         ),
         in_specs=[
-            pl.BlockSpec(memory_space=V),
+            pl.BlockSpec(memory_space=pl.ANY),
             pl.BlockSpec(memory_space=pl.ANY),
             pl.BlockSpec(memory_space=pl.ANY),
             pl.BlockSpec(memory_space=pl.ANY),
@@ -413,7 +456,17 @@
             collective_id=0, has_side_effects=True, vmem_limit_bytes=56 * 1024 * 1024
         ),
         name="distill",
-    )(hidden, head_weight, teacher_logprobs, lengths)
+    )(hidden, head_weight, teacher_logprobs, lengths.T)
+    return pl.pallas_call(
+        hand_over,
+        out_shape=(
+            jax.ShapeDtypeStruct(grad.shape, grad.dtype),
+            jax.ShapeDtypeStruct(divergence.shape, divergence.dtype),
+        ),
+        in_specs=[pl.BlockSpec(memory_space=V)] * 2,
+        out_specs=(pl.BlockSpec(memory_space=V), pl.BlockSpec(memory_space=V)),
+        name="hand_over",
+    )(grad, divergence)
 
 
 def solution(mesh):

time: 82.3 us -> 76.1 us (0.925)
  the two profiles are of different devices: /device:TPU:1 before, /device:TPU:32 now
where the time goes in v3:
time: 76.1 us; the launch traced here: 76 us
  Pallas kernels  75.3 us (99%)
    pallas_call x1, Pallas kernels, body(): pl.pallas_call(kernel, out_shape=(jax.ShapeDtypeStruct((1, 8, width), BF1...  74 us

profile of v3, /device:TPU:32, one launch (start us, length us, event | category | flops | bytes accessed | tf_op | source)
XLA Modules:
  0.0 76.0 jit_solution(10209189152000246619)
XLA Ops:
  0.6 74.0 %distill.1 = (bf16[1,8,1792]{2,1,0:T(8,128)(2,1)}, f32[1,64]{1,0:T(1,128)}) custom-call(bf16[1,8,1792]{2,1,0:T(8,128)(2,1)} %hid_hbm.1, bf16[1792,640]{1,0:T(8,128)(2,1)} %w_hbm.1, f32[8,64,640]{2,1,0:T(8,128)} %tl_hbm.1, s32[4,8]{1,0:T(4,128)} %bitcast.1), custom_call_target="tpu_custom_call" | custom-call | tf_op jit(solution)/shard_map/distill/pallas_call | solution.py:441
  74.6 1.4 %hand_over.1 = (bf16[1,8,1792]{2,1,0:T(8,128)(2,1)}, f32[1,64]{1,0:T(1,128)}) custom-call(bf16[1,8,1792]{2,1,0:T(8,128)(2,1)} %get-tuple-element.4.grad_ref, f32[1,64]{1,0:T(1,128)} %get-tuple-element.5.div_ref), custom_call_target="tpu_custom_call" | custom-call | tf_op jit(solution)/shard_map/hand_over/pallas_call | solution.py:460

commit v4 on v3

--- a/solution.py
+++ b/solution.py
@@ -7,17 +7,17 @@
 
 SEQ_MB = 32
 NX, NY, NZ = 4, 4, 8
-NA, NB = 512, 768
+NA, NC, NB = 640, 512, 640
 F32, BF16 = jnp.float32, jnp.bfloat16
 
 
 def kernel(
     hid_hbm, w_hbm, tl_hbm, len_hbm, grad_ref, div_ref,
     w, tl, tp, lengths, zb, pb, hb, bz, acc, lrecv, stats, rz, rp, g,
-    s1, f1, own1, r1h, r1f, s2, r2, u, s3, r3, prod, sb, rb, s4, r4,
+    s1, f1, own1, r1h, sd, r1f, s2, r2, u, s3, r3, prod, sb, rb, s4, r4,
     lsem, ssem, rsem,
 ):
-    wide = NA + NA
+    wide = NA + NC
     vocab = w.shape[1]
     section, z, t = lax.axis_index("section"), lax.axis_index("dp"), lax.axis_index("tensor")
     x, y = section // NY, section % NY
@@ -58,7 +58,7 @@
     for peer in peers:
         pl.semaphore_signal(barrier, inc=1, device_id=peer, device_id_type=pl.DeviceIdType.MESH)
 
-    ca, cc, cac, cb = pl.ds(0, NA), pl.ds(NA, NA), pl.ds(0, wide), pl.ds(wide, NB)
+    ca, cc, cac, cb = pl.ds(0, NA), pl.ds(NA, NC), pl.ds(0, wide), pl.ds(wide, NB)
     own_rows = (
         pltpu.make_async_copy(hid_hbm.at[0, :, cac], zb.at[z], lsem.at[10]),
         pltpu.make_async_copy(hid_hbm.at[0, :, cb], pb.at[section], lsem.at[11]),
@@ -81,10 +81,39 @@
     for copy in zs:
         copy.wait_recv()
     hb[x, y] = zb[...].astype(F32).reshape(NZ * 8, wide).astype(BF16)
-    ph2 = []
+
+    def a_at(xx, k):
+        return hb.at[(x + xx) % NX, (y + k) % NY, :, ca]
+
+    def c_at(yy, k):
+        return hb.at[(x + k) % NX, (y + yy) % NY, :, cc]
+
+    blocks = (a_at, c_at)
+    along = (at_x, at_y)
+    across = (at_y, at_x)
+
+    def odd(part, k):
+        return ((y, x)[part] + k) % 2
+
+    spread, near, passed = {}, {}, {}
+
+    def send_near(part, k):
+        block = blocks[part](0, k)
+        near[part, k] = (send(block, block, along[part](1)), send(block, block, along[part](3)))
+
+    def pass_on(part, k):
+        for copy in near[part, k]:
+            copy.wait_recv()
+        back = 2 * odd(part, k)
+        block = blocks[part](3 + back, k)
+        passed[part, k] = send(block, block, along[part](1 + back))
+
     for k in (2, 1, 3):
-        ph2.append(send(hb.at[x, y, :, ca], hb.at[x, y, :, ca], at_y(k)))
-        ph2.append(send(hb.at[x, y, :, cc], hb.at[x, y, :, cc], at_x(k)))
+        for part in range(2):
+            block = blocks[part](0, 0)
+            spread[part, k] = send(block, block, across[part](k))
+    for part in range(2):
+        send_near(part, 0)
     for copy in ps:
         copy.wait_recv()
     bz[z] = pb[...].astype(F32).reshape(128, NB).astype(BF16)
@@ -102,43 +131,43 @@
         right = which in (0, 2)
         ring[step].append(b_pass(step, right, top_half if which in (0, 3) else low_half))
 
+    for k in (1, 3):
+        for part in range(2):
+            spread[part, k].wait_recv()
+            send_near(part, 4 - k)
     ring.append([])
     for which in range(4):
         b_forward(1, which)
-
-    for copy in ph2:
-        copy.wait_recv()
-    y1, y3, x1, x3 = (y + 1) % NY, (y + 3) % NY, (x + 1) % NX, (x + 3) % NX
-    lo2, hi2 = pl.ds(0, 2), pl.ds(2, 2)
-
-    def a_block(i, part):
-        return hb.at[i, part, :, ca]
-
-    def c_block(i, part):
-        return hb.at[part, i, :, cc]
-
-    ar0 = send(a_block(x, lo2), a_block(x, lo2), at_x(1))
-    br0 = send(c_block(y, lo2), c_block(y, lo2), at_y(1))
-    al0 = send(a_block(x, hi2), a_block(x, hi2), at_x(3))
-    bl0 = send(c_block(y, hi2), c_block(y, hi2), at_y(3))
-    ar1 = send(a_block(x, hi2), a_block(x, hi2), at_x(1))
-    br1 = send(c_block(y, hi2), c_block(y, hi2), at_y(1))
-    al1 = send(a_block(x, lo2), a_block(x, lo2), at_x(3))
-    bl1 = send(c_block(y, lo2), c_block(y, lo2), at_y(3))
-
+    for part in range(2):
+        spread[part, 2].wait_recv()
+        send_near(part, 2)
+    for part in range(2):
+        pass_on(part, 0)
     def a_logits(i):
         rows = hb[i, :, :, 0:NA].reshape(256, NA)
         block = jnp.dot(rows, w[0:NA], preferred_element_type=F32)
         acc[i] = acc[i] + block.reshape(4, 8, 8, vocab)
 
     def c_logits(i):
-        rows = hb[:, i, :, NA:wide].reshape(256, NA)
+        rows = hb[:, i, :, NA:wide].reshape(256, NC)
         block = jnp.dot(rows, w[NA:wide], preferred_element_type=F32)
         acc[:, i] = acc[:, i] + block.reshape(4, 8, 8, vocab)
 
     def b_logits(i):
         block = jnp.dot(bz[i], w[wide:], preferred_element_type=F32)
         acc[:, :, i] = acc[:, :, i] + block.reshape(4, 4, 8, vocab)
+
+    def c_far(owner):
+        rows = hb[pl.ds(2 * owner, 2), (y + 2) % NY, :, NA:wide].reshape(128, NC)
+        block = jnp.dot(rows, w[NA:wide], preferred_element_type=F32)
+        into = acc.at[pl.ds(2 * owner, 2), (y + 2) % NY]
+        into[...] = into[...] + block.reshape(2, 8, 8, vocab)
+
+    def b_far(owner):
+        rows = bz[(z + 4) % NZ, pl.ds(pl.multiple_of(64 * owner, 64), 64), :]
+        block = jnp.dot(rows, w[wide:], preferred_element_type=F32)
+        into = acc.at[pl.ds(2 * owner, 2), :, (z + 4) % NZ]
+        into[...] = into[...] + block.reshape(2, 4, 8, vocab)
 
     for load in loads:
         load.wait()
@@ -151,47 +180,43 @@
     b_logits(z)
     a_logits(x)
     c_logits(y)
-
+    for k in (1, 3):
+        for part in range(2):
+            pass_on(part, k)
     ring.append([])
     for which in range(4):
         b_forward(2, which)
     b_logits((z + 1) % NZ)
     b_logits((z + 7) % NZ)
-    ar0.wait_recv()
-    ar2 = send(a_block(x3, lo2), a_block(x3, lo2), at_x(1))
-    br0.wait_recv()
-    br2 = send(c_block(y3, lo2), c_block(y3, lo2), at_y(1))
-    al0.wait_recv()
-    al2 = send(a_block(x1, hi2), a_block(x1, hi2), at_x(3))
-    bl0.wait_recv()
-    bl2 = send(c_block(y1, hi2), c_block(y1, hi2), at_y(3))
+    for part in range(2):
+        pass_on(part, 2)
+    for k in (1, 3):
+        a_logits((x + k) % NX)
+        c_logits((y + k) % NY)
     ring.append([])
     for which in range(2):
         b_forward(3, which)
     b_logits((z + 2) % NZ)
     b_logits((z + 6) % NZ)
-    for copy in [ar1, br1, al1, bl1]:
-        copy.wait_recv()
-    for k in (1, 3):
-        a_logits((x + k) % NX)
-        c_logits((y + k) % NY)
     for copy in ring[2][2:4]:
         copy.wait_recv()
     b_logits((z + 3) % NZ)
     b_logits((z + 5) % NZ)
-    for copy in (ar2, al2):
-        copy.wait_recv()
+    for k in range(4):
+        passed[0, k].wait_recv()
     a_logits((x + 2) % NX)
-    for copy in (br2, bl2):
-        copy.wait_recv()
-    c_logits((y + 2) % NY)
+    for k in range(4):
+        passed[1, k].wait_recv()
     for copy in ring[3]:
         copy.wait_recv()
-    b_logits((z + 4) % NZ)
+    c_far(other)
+    b_far(other)
     exchanges = []
     for k in range(4):
         block = acc.at[2 * other + k // 2, pl.ds(2 * (k % 2), 2)]
         exchanges.append(send(block, lrecv.at[pl.ds(2 * k, 2)], partner))
+    c_far(t)
+    b_far(t)
 
     row_i = lax.broadcasted_iota(jnp.int32, (128, 128), 0)
     lane_i = lax.broadcasted_iota(jnp.int32, (128, 128), 1)
@@ -280,15 +305,17 @@
     def product(part, o):
         rows = g[(x + o) % NX] if part == 0 else g[:, (y + o) % NY]
         rows = rows.astype(F32).reshape(256, vocab).astype(BF16)
-        return times_w(rows, part * NA, NA).reshape(4, 64, NA)
+        return times_w(rows, (0, NA)[part], size[part]).reshape(4, 64, size[part])
 
     def b_product(o):
         i = (z + o) % NZ
         rows = g[:, :, i].astype(F32).reshape(128, vocab).astype(BF16)
         prod[i] = times_w(rows, wide, NB)
 
-    first = (at_x, at_y)
-    second = (at_y, at_x)
+    size = (NA, NC)
+    fit = (pl.ds(0, NA), pl.ds(0, NC))
+    mine = (y, x)
+    order = (2, 1, 3, 0)
     halves = (slice(0, 64), slice(64, 128))
 
     def b_item(side, item, extra=None):
@@ -301,15 +328,16 @@
         sb[side, item] = value.astype(BF16)
         return send(sb.at[side, item], rb.at[side, item], at_z(1 if side == 0 else NZ - 1))
 
-    hop, direct = [], []
+    hop, direct = {}, {}
     b_product(4)
     sides = [[b_item(side, 0)] for side in range(2)]
     for part in range(2):
-        s1[part, 2] = product(part, 2).astype(BF16)
-        hop.append((
-            send(s1.at[part, 2, lo2], r1h.at[part, 0], first[part](1)),
-            send(s1.at[part, 2, hi2], r1h.at[part, 1], first[part](3)),
-        ))
+        s1[part, :, :, fit[part]] = product(part, 2).astype(BF16)
+        for k in order:
+            back = 2 * odd(part, k)
+            hop[part, k] = send(
+                s1.at[part, (mine[part] + k) % 4, :, fit[part]], r1h.at[part, k, :, fit[part]], along[part](1 + back)
+            )
     for side in range(2):
         b_product((3, 5)[side])
         sides[side].append(b_item(side, 1))
@@ -321,51 +349,64 @@
             sides[side].append(b_item(side, item, rb[side, source].astype(F32)))
 
     for part in range(2):
-        block = product(part, 1)
-        f1[part, 0] = block[0:2]
-        s1[part, 1, 2:4] = block[2:4].astype(BF16)
-        direct.append(send(s1.at[part, 1, hi2], r1f.at[part, 0, hi2], first[part](1)))
-        block = product(part, 3)
-        f1[part, 1] = block[2:4]
-        s1[part, 3, 0:2] = block[0:2].astype(BF16)
-        direct.append(send(s1.at[part, 3, lo2], r1f.at[part, 1, lo2], first[part](3)))
+        f1[part, 0, :, :, fit[part]] = product(part, 1)
+        f1[part, 1, :, :, fit[part]] = product(part, 3)
+        for k in order:
+            back = odd(part, k)
+            sd[part, 0, k, :, fit[part]] = f1[part, 1 - back, (mine[part] + k) % 4, :, fit[part]].astype(BF16)
+            direct[part, 0, k] = send(
+                sd.at[part, 0, k, :, fit[part]], r1f.at[part, 0, k, :, fit[part]], along[part](3 - 2 * back)
+            )
     b_next(2)
     b_product(2)
     b_product(6)
-    for part in range(2):
-        hop[part][0].wait_recv()
-        s1[part, 1, 0:2] = (f1[part, 0] + r1h[part, 0].astype(F32)).astype(BF16)
-        direct.append(send(s1.at[part, 1, lo2], r1f.at[part, 0, lo2], first[part](1)))
-        hop[part][1].wait_recv()
-        s1[part, 3, 2:4] = (f1[part, 1] + r1h[part, 1].astype(F32)).astype(BF16)
-        direct.append(send(s1.at[part, 3, hi2], r1f.at[part, 1, hi2], first[part](3)))
+    for k in order:
+        for part in range(2):
+            hop[part, k].wait_recv()
+            back = odd(part, k)
+            value = f1[part, back, (mine[part] + k) % 4, :, fit[part]] + r1h[part, k, :, fit[part]].astype(F32)
+            sd[part, 1, k, :, fit[part]] = value.astype(BF16)
+            direct[part, 1, k] = send(
+                sd.at[part, 1, k, :, fit[part]], r1f.at[part, 1, k, :, fit[part]], along[part](1 + 2 * back)
+            )
     b_next(3)
     b_product(1)
     b_product(7)
     b_product(0)
     for part in range(2):
-        own1[part] = product(part, 0)
+        own1[part, :, :, fit[part]] = product(part, 0)
     b_next(4)
+
+    def whole(part, k):
+        direct[part, 0, k].wait_recv()
+        direct[part, 1, k].wait_recv()
+        value = own1[part, (mine[part] + k) % 4, :, fit[part]]
+        return value + r1f[part, 0, k, :, fit[part]].astype(F32) + r1f[part, 1, k, :, fit[part]].astype(F32)
+
+    ph2 = []
+
+    def second(k):
+        for part in range(2):
+            s2[part, k - 1, :, fit[part]] = whole(part, k).astype(BF16)
+            ph2.append(send(
+                s2.at[part, k - 1, :, fit[part]], r2.at[part, k - 1, :, fit[part]], across[part](k)
+            ))
+
+    second(2)
     b_next(5)
-    for copy in direct:
-        copy.wait_recv()
-    place2 = (y, x)
-    ph2 = []
-    for k in (2, 1, 3):
-        for part in range(2):
-            i = (place2[part] + k) % 4
-            value = own1[part, i] + r1f[part, 0, i].astype(F32) + r1f[part, 1, i].astype(F32)
-            s2[part, k - 1] = value.astype(BF16)
-            ph2.append(send(s2.at[part, k - 1], r2.at[part, k - 1], second[part](k)))
+    second(1)
+    second(3)
+    for part in range(2):
+        own1[part, mine[part], :, fit[part]] = whole(part, 0)
     b_next(6)
     for copy in ph2:
         copy.wait_recv()
     for part in range(2):
-        i = place2[part]
-        value = own1[part, i] + r1f[part, 0, i].astype(F32) + r1f[part, 1, i].astype(F32)
+        value = own1[part, mine[part], :, fit[part]]
         for k in range(3):
-            value = value + r2[part, k].astype(F32)
-        u[:, :, part * NA:(part + 1) * NA] = value.reshape(NZ, 8, NA)
+            value = value + r2[part, k, :, fit[part]].astype(F32)
+        start = (0, NA)[part]
+        u[:, :, start:start + size[part]] = value.reshape(NZ, 8, size[part])
     s3[...] = u[...].astype(BF16)
     zs = [send(s3.at[(z + k) % NZ], r3.at[k - 1], at_z(k)) for k in far_z]
     for side in range(2):
@@ -397,12 +438,12 @@
     div_out[...] = div_ref[...]
 
 
-N_SEM = 160
+N_SEM = 176
 
 
 def body(hidden, head_weight, teacher_logprobs, lengths):
     width, vocab = head_weight.shape
-    wide = 2 * NA
+    wide = NA + NC
     V = pltpu.VMEM
     scratch = [
         V((width, vocab), BF16),
@@ -419,10 +460,11 @@
         V((NZ - 1, 16, 128), F32),
         V((15, 16, 128), F32),
         V((NX, NY, 8, 8, vocab), BF16),
-        V((2, 4, 4, 64, NA), BF16),
-        V((2, 2, 2, 64, NA), F32),
+        V((2, 4, 64, NA), BF16),
+        V((2, 2, 4, 64, NA), F32),
         V((2, 4, 64, NA), F32),
-        V((2, 2, 2, 64, NA), BF16),
+        V((2, 4, 64, NA), BF16),
+        V((2, 2, 4, 64, NA), BF16),
         V((2, 2, 4, 64, NA), BF16),
         V((2, 3, 64, NA), BF16),
         V((2, 3, 64, NA), BF16),

time: 76.1 us -> 77.9 us (1.024)
  the two profiles are of different devices: /device:TPU:32 before, /device:TPU:1 now
where the time goes in v4:
time: 77.9 us; the launch traced here: 77.7 us
  Pallas kernels  77.1 us (99%)
    pallas_call x1, Pallas kernels, body(): pl.pallas_call(kernel, out_shape=(jax.ShapeDtypeStruct((1, 8, width), BF1...  75.7 us

profile of v4, /device:TPU:1, one launch (start us, length us, event | category | flops | bytes accessed | tf_op | source)
XLA Modules:
  0.0 77.7 jit_solution(11507051177286675661)
XLA Ops:
  0.6 75.7 %distill.1 = (bf16[1,8,1792]{2,1,0:T(8,128)(2,1)}, f32[1,64]{1,0:T(1,128)}) custom-call(bf16[1,8,1792]{2,1,0:T(8,128)(2,1)} %hid_hbm.1, bf16[1792,640]{1,0:T(8,128)(2,1)} %w_hbm.1, f32[8,64,640]{2,1,0:T(8,128)} %tl_hbm.1, s32[4,8]{1,0:T(4,128)} %bitcast.1), custom_call_target="tpu_custom_call" | custom-call | tf_op jit(solution)/shard_map/distill/pallas_call | solution.py:483
  76.4 1.4 %hand_over.1 = (bf16[1,8,1792]{2,1,0:T(8,128)(2,1)}, f32[1,64]{1,0:T(1,128)}) custom-call(bf16[1,8,1792]{2,1,0:T(8,128)(2,1)} %get-tuple-element.4.grad_ref, f32[1,64]{1,0:T(1,128)} %get-tuple-element.5.div_ref), custom_call_target="tpu_custom_call" | custom-call | tf_op jit(solution)/shard_map/hand_over/pallas_call | solution.py:502

commit v5 on v0

v5 whole, which is shorter than its diff:
```python
import jax
import jax.numpy as jnp
from jax import lax
from jax.experimental import pallas as pl
from jax.experimental.pallas import tpu as pltpu
from jax.sharding import PartitionSpec as P

SEQ_MB, LIVE = 32, 80
NX, NY, NZ = 4, 4, 8
CH, NB = 128, 768
HB = NB // 2
F32, BF16 = jnp.float32, jnp.bfloat16


def kernel(
    hid_hbm, w_hbm, tl_hbm, len_hbm, grad_ref, div_ref,
    w, hid, trow, tlc, tp, lengths, pk, p1, ha, hc, hz, acc, lrecv, stats, rz, rp, dv, g,
    sa, fa, own, rah, sd, raf, s3, r3, prod, sb, rb, pk2, r4, oa, oc,
    lsem, ssem, rsem,
):
    vocab = w.shape[2]
    rows = NZ * LIVE
    section, z, t = lax.axis_index("section"), lax.axis_index("dp"), lax.axis_index("tensor")
    x, y = section // NY, section % NY
    other = 1 - t

    def at_x(k):
        return (((x + k) % NX) * NY + y, z, t)

    def at_y(k):
        return (x * NY + (y + k) % NY, z, t)

    def at_z(k):
        return (section, (z + k) % NZ, t)

    def plane(k):
        return ((x + k // NY) % NX) * NY + (y + k % NY) % NY

    def at_p(k):
        return (plane(k), z, t)

    far_z = (4, 3, 5, 2, 6, 1, 7)
    far_p = (10, 6, 14, 9, 11, 2, 8, 5, 7, 13, 15, 1, 3, 4, 12)
    partner = (section, z, other)
    started = []

    def send(src, dst, device):
        i = len(started)
        copy = pltpu.make_async_remote_copy(
            src_ref=src, dst_ref=dst, send_sem=ssem.at[i], recv_sem=rsem.at[i],
            device_id=device, device_id_type=pl.DeviceIdType.MESH,
        )
        copy.start()
        started.append(copy)
        return copy

    barrier = pltpu.get_barrier_semaphore()
    peers = [at_z(k) for k in far_z] + [at_p(k) for k in far_p] + [partner]
    for peer in peers:
        pl.semaphore_signal(barrier, inc=1, device_id=peer, device_id_type=pl.DeviceIdType.MESH)

    load_hid = pltpu.make_async_copy(hid_hbm.at[0], hid, lsem.at[0])
    load_len = pltpu.make_async_copy(len_hbm, lengths, lsem.at[1])
    load_w = pltpu.make_async_copy(w_hbm, w, lsem.at[2])
    load_tl = pltpu.make_async_copy(tl_hbm.at[pl.ds(4 * t, 4)], trow.at[:, t], lsem.at[3])
    for load in (load_hid, load_len, load_w, load_tl):
        load.start()
    load_hid.wait()
    for p in range(NX * NY):
        a0, c0 = (p // NY) * CH, (NX + p % NY) * CH
        pk[p] = jnp.concatenate([hid[:, a0:a0 + CH], hid[:, c0:c0 + CH], hid[:, 8 * CH:]], axis=1)
    pl.semaphore_wait(barrier, len(peers))

    ps = [send(pk.at[plane(k)], p1.at[section], at_p(k)) for k in far_p]
    teacher_swap = send(tl_hbm.at[pl.ds(4 * other, 4)], trow.at[:, t], partner)
    p1[section] = pk[section]
    acc[...] = jnp.zeros_like(acc)
    load_len.wait()

    def ends(r):
        first = lengths[0, r]
        second = first + lengths[1, r]
        return first, second, second + lengths[2, r]

    def position(r, j):
        e1, e2, e3 = ends(r)
        late = jnp.where(j >= e3, 3 * SEQ_MB - e3, 2 * SEQ_MB - e2)
        early = jnp.where(j >= e1, SEQ_MB - e1, 0)
        return j + jnp.where(j >= e2, late, early)

    row_j = lax.broadcasted_iota(jnp.int32, (LIVE, 128), 0)
    lane_p = lax.broadcasted_iota(jnp.int32, (LIVE, 128), 1)
    eye = row_j == lane_p

    def picker(r):
        return (lane_p == position(r, row_j)).astype(F32).astype(BF16)

    pick_z = picker(z)
    for copy in ps:
        copy.wait_recv()
    block = p1[...].astype(F32).reshape(128, 2 * CH + NB).astype(BF16)
    block = jnp.dot(pick_z, block, preferred_element_type=F32).astype(BF16)
    ha[x, z] = block[:, 0:CH]
    hc[y, z] = block[:, CH:2 * CH]
    hz[z] = block[:, 2 * CH:]

    def b_pass(step, right):
        i = (z - step) % NZ if right else (z + step) % NZ
        part = hz.at[i] if step < 3 else hz.at[i, :, pl.ds(0 if right else HB, HB)]
        return send(part, part, at_z(1 if right else NZ - 1))

    ring = [(b_pass(0, True), b_pass(0, False))]
    zs = []
    for k in far_z:
        zs.append(send(ha.at[x, z], ha.at[x, z], at_z(k)))
        zs.append(send(hc.at[y, z], hc.at[y, z], at_z(k)))

    def b_forward(step):
        ring[step - 1][0].wait_recv()
        right = b_pass(step, True)
        ring[step - 1][1].wait_recv()
        ring.append((right, b_pass(step, False)))

    load_w.wait()

    def b_logits(i):
        low = w[2 * NX:].reshape(NB, vocab)
        acc[i] = acc[i] + jnp.dot(hz[i], low, preferred_element_type=F32)

    def ac_logits(chunks, start, count):
        left = [ha[(x + k) % NX, pl.ds(start, count)].reshape(count * LIVE, CH) for k in chunks]
        left += [hc[(y + k) % NY, pl.ds(start, count)].reshape(count * LIVE, CH) for k in chunks]
        right = [w[(x + k) % NX] for k in chunks] + [w[NX + (y + k) % NY] for k in chunks]
        block = jnp.dot(
            jnp.concatenate(left, axis=1), jnp.concatenate(right, axis=0), preferred_element_type=F32
        )
        into = acc.at[pl.ds(start, count)]
        into[...] = into[...] + block.reshape(count, LIVE, vocab)

    load_tl.wait()
    teacher_swap.wait_recv()
    for r in range(4):
        pick = picker(4 * t + r)
        rest = trow[r].reshape(128, vocab)
        total = None
        for _ in range(3):
            piece = rest.astype(BF16)
            rest = rest - piece.astype(F32)
            part = jnp.dot(pick, piece, preferred_element_type=F32)
            total = part if total is None else total + part
        tlc[r] = total
        tp[r] = jnp.exp(total)

    b_forward(1)
    b_logits(z)
    for copy in zs:
        copy.wait_recv()
    near = (
        send(ha.at[x], ha.at[x], at_x(1)), send(hc.at[y], hc.at[y], at_y(1)),
        send(ha.at[x], ha.at[x], at_x(3)), send(hc.at[y], hc.at[y], at_y(3)),
    )
    b_logits((z + 1) % NZ)
    b_logits((z + 7) % NZ)
    b_forward(2)
    b_logits((z + 2) % NZ)
    b_logits((z + 6) % NZ)
    upper, lower = pl.ds(0, 4), pl.ds(4, 4)
    x1, x3, y1, y3 = (x + 1) % NX, (x + 3) % NX, (y + 1) % NY, (y + 3) % NY
    passed = []
    for copy, buf, i, half, device in (
        (near[0], ha, x3, upper, at_x(1)), (near[1], hc, y3, upper, at_y(1)),
        (near[2], ha, x1, lower, at_x(3)), (near[3], hc, y1, lower, at_y(3)),
    ):
        copy.wait_recv()
        passed.append(send(buf.at[i, half], buf.at[i, half], device))
    b_forward(3)
    ac_logits((0, 1, 3), 0, NZ)
    b_logits((z + 3) % NZ)
    b_logits((z + 5) % NZ)
    for copy in passed:
        copy.wait_recv()
    ac_logits((2,), 4 * other, 4)
    for copy in ring[3]:
        copy.wait_recv()
    b_logits((z + 4) % NZ)
    exchanges = []
    for k in range(4):
        exchanges.append(send(acc.at[4 * other + k], lrecv.at[k], partner))
    ac_logits((2,), 4 * t, 4)

    def to_lanes(col):
        return jnp.sum(jnp.where(eye, col, 0.0), axis=0, keepdims=True)

    def to_rows(lane):
        return jnp.sum(jnp.where(eye, lane, 0.0), axis=1, keepdims=True)

    for k in range(4):
        exchanges[k].wait_recv()
        logits = acc[4 * t + k] + lrecv[k]
        lrecv[k] = logits
        prob = tp[k]
        top = jnp.max(logits, axis=1, keepdims=True)
        total = jnp.sum(jnp.exp(logits - top), axis=1, keepdims=True)
        cross = jnp.sum(prob * (tlc[k] - logits), axis=1, keepdims=True)
        mass = jnp.sum(prob, axis=1, keepdims=True)
        stats[0, k:k + 1, :] = to_lanes(top)
        stats[0, 4 + k:5 + k, :] = to_lanes(total)
        stats[0, 8 + k:9 + k, :] = to_lanes(cross)
        stats[0, 12 + k:13 + k, :] = to_lanes(mass)

    for level, (slots, at, order) in enumerate(((rz, at_z, far_z), (rp, at_p, far_p))):
        copies = [send(stats.at[level], slots.at[k - 1], at(k)) for k in order]
        for copy in copies:
            copy.wait_recv()
        parts = [stats[level]] + [slots[k] for k in range(len(order))]
        top = parts[0][0:4]
        for part in parts[1:]:
            top = jnp.maximum(top, part[0:4])
        total = sum(part[4:8] * jnp.exp(part[0:4] - top) for part in parts)
        sums = sum(part[8:16] for part in parts)
        stats[level + 1, 0:4, :] = top
        stats[level + 1, 4:8, :] = total
        stats[level + 1, 8:16, :] = sums

    row_r = lax.broadcasted_iota(jnp.int32, (4, 128), 0)
    lane_j = lax.broadcasted_iota(jnp.int32, (4, 128), 1)
    log_norm = stats[2, 0:4, :] + jnp.log(jnp.where(lane_j < LIVE, stats[2, 4:8, :], 1.0))
    cross, mass = stats[2, 8:12, :], stats[2, 12:16, :]
    chosen = jnp.ones((4, 128), jnp.int32)
    for r in range(4):
        e1, e2, e3 = ends(4 * t + r)
        late = jnp.where(lane_j >= e3, lengths[3, 4 * t + r], lengths[2, 4 * t + r])
        early = jnp.where(lane_j >= e1, lengths[1, 4 * t + r], lengths[0, 4 * t + r])
        chosen = jnp.where(row_r == r, jnp.where(lane_j >= e2, late, early), chosen)
    weight = SEQ_MB / chosen.astype(F32)
    dv[t] = cross + log_norm * mass
    scale = weight * mass

    swaps = []
    for k in range(4):
        norm_rows = to_rows(log_norm[k:k + 1])
        scale_rows = to_rows(scale[k:k + 1])
        weight_rows = to_rows(weight[k:k + 1])
        grad = jnp.exp(lrecv[k] - norm_rows) * scale_rows - weight_rows * tp[k]
        g[4 * t + k] = grad.astype(BF16)
        swaps.append(send(g.at[4 * t + k], g.at[4 * t + k], partner))
    share = send(dv.at[t], dv.at[t], partner)
    for copy in swaps:
        copy.wait_recv()

    def times_w(left, right):
        return lax.dot_general(left, right, (((1,), (1,)), ((), ())), preferred_element_type=F32)

    def product(part, o):
        chunk = w[(x + o) % NX] if part == 0 else w[NX + (y + o) % NY]
        return times_w(g[...].reshape(rows, vocab), chunk)

    along = (at_x, at_y)
    cut = rows // 2

    def b_item(side, item, extra=None):
        step = 0 if item == 0 else (item + 1) // 2
        first = (item % 2 == 0) if side == 0 else (item % 2 == 1)
        owner = (z + 4 - step) % NZ if side == 0 else (z + 4 + step) % NZ
        value = prod[owner, :, 0:HB] if first else prod[owner, :, HB:NB]
        if extra is not None:
            value = value + extra
        sb[side, item] = value.astype(BF16)
        return send(sb.at[side, item], rb.at[side, item], at_z(1 if side == 0 else NZ - 1))

    def b_next(item):
        source = item - 2
        for side in range(2):
            sides[side][source].wait_recv()
            sides[side].append(b_item(side, item, rb[side, source].astype(F32)))

    low = w[2 * NX:].reshape(NB, vocab)
    prod[(z + 4) % NZ] = times_w(g[(z + 4) % NZ], low)
    sides = [[b_item(side, 0)] for side in range(2)]
    hop, direct = [], []
    for part in range(2):
        sa[part] = product(part, 2).astype(BF16)
        hop.append((
            send(sa.at[part, pl.ds(0, cut)], rah.at[part, 0], along[part](1)),
            send(sa.at[part, pl.ds(cut, cut)], rah.at[part, 1], along[part](3)),
        ))
    prod[...] = times_w(g[...].reshape(rows, vocab), low).reshape(NZ, LIVE, NB)
    for side in range(2):
        sides[side].append(b_item(side, 1))
    for part in range(2):
        for d, o in ((0, 1), (1, 3)):
            block = product(part, o)
            fa[part, d] = block[d * cut:(d + 1) * cut]
            sd[part, d, 1 - d] = block[(1 - d) * cut:(2 - d) * cut].astype(BF16)
            direct.append(send(sd.at[part, d, 1 - d], raf.at[part, d, 1 - d], along[part](o)))
    b_next(2)
    for part in range(2):
        own[part] = product(part, 0)
    for part in range(2):
        for d, o in ((0, 1), (1, 3)):
            hop[part][d].wait_recv()
            sd[part, d, d] = (fa[part, d] + rah[part, d].astype(F32)).astype(BF16)
            direct.append(send(sd.at[part, d, d], raf.at[part, d, d], along[part](o)))
    b_next(3)
    b_next(4)
    for copy in direct:
        copy.wait_recv()
    for part in range(2):
        for h in range(2):
            piece = pl.ds(h * cut, cut)
            value = own[part, piece] + raf[part, 0, h].astype(F32) + raf[part, 1, h].astype(F32)
            own[part, piece] = value
            s3[4 * h:4 * h + 4, :, part * CH:(part + 1) * CH] = value.reshape(4, LIVE, CH).astype(BF16)
    zs = [send(s3.at[(z + k) % NZ], r3.at[k - 1], at_z(k)) for k in far_z]
    b_next(5)
    b_next(6)
    share.wait_recv()
    mine = jnp.sum(jnp.where(row_r == z % 4, dv[z // 4], 0.0), axis=0, keepdims=True)
    placed = lane_p + 64 * t == position(z, row_j)
    div_ref[...] = jnp.sum(jnp.where(placed, to_rows(mine), 0.0), axis=0, keepdims=True)[:, 0:64]
    for side in range(2):
        for item in (5, 6):
            sides[side][item].wait_recv()
    b_first = prod[z, :, 0:HB] + rb[0, 6].astype(F32) + rb[1, 5].astype(F32)
    b_second = prod[z, :, HB:NB] + rb[0, 5].astype(F32) + rb[1, 6].astype(F32)
    for copy in zs:
        copy.wait_recv()
    start = pl.multiple_of(z * LIVE, LIVE)
    ac = jnp.concatenate([own[0, pl.ds(start, LIVE)], own[1, pl.ds(start, LIVE)]], axis=1)
    for k in range(NZ - 1):
        ac = ac + r3[k].astype(F32)
    live = jnp.concatenate([ac.astype(BF16), b_first.astype(BF16), b_second.astype(BF16)], axis=1)
    spread_p = lax.broadcasted_iota(jnp.int32, (128, LIVE), 0)
    spread_j = lax.broadcasted_iota(jnp.int32, (128, LIVE), 1)
    spread = (spread_p == position(z, spread_j)).astype(F32).astype(BF16)
    full = jnp.dot(spread, live, preferred_element_type=F32)
    pk2[...] = full.reshape(NX * NY, 8, 2 * CH + NB).astype(BF16)
    ps = [send(pk2.at[plane(k)], r4.at[k - 1], at_p(k)) for k in far_p]
    for copy in ps:
        copy.wait_recv()
    parts = [pk2[section].astype(F32)] + [r4[k].astype(F32) for k in range(15)]
    for i in range(4):
        oa[(x + NX - i) % NX] = sum(parts[NY * i + j][:, 0:CH] for j in range(4))
        oc[(y + NY - i) % NY] = sum(parts[NY * j + i][:, CH:2 * CH] for j in range(4))
    grad_ref[0, :, 2 * NX * CH:] = sum(part[:, 2 * CH:] for part in parts).astype(BF16)
    for i in range(4):
        grad_ref[0, :, i * CH:(i + 1) * CH] = oa[i].astype(BF16)
        grad_ref[0, :, (NX + i) * CH:(NX + i + 1) * CH] = oc[i].astype(BF16)

    for copy in started:
        copy.wait_send()


def hand_over(grad_ref, div_ref, grad_out, div_out):
    grad_out[...] = grad_ref[...]
    div_out[...] = div_ref[...]


N_SEM = 144


def body(hidden, head_weight, teacher_logprobs, lengths):
    width, vocab = head_weight.shape
    V = pltpu.VMEM
    packed = 2 * CH + NB
    rows = NZ * LIVE
    scratch = [
        V((width // CH, CH, vocab), BF16),
        V((8, width), BF16),
        V((4, 2, 64, vocab), F32),
        V((4, LIVE, vocab), F32),
        V((4, LIVE, vocab), F32),
        pltpu.SMEM((4, 8), jnp.int32),
        V((16, 8, packed), BF16),
        V((16, 8, packed), BF16),
        V((NX, NZ, LIVE, CH), BF16),
        V((NY, NZ, LIVE, CH), BF16),
        V((NZ, LIVE, NB), BF16),
        V((NZ, LIVE, vocab), F32),
        V((4, LIVE, vocab), F32),
        V((3, 16, 128), F32),
        V((NZ - 1, 16, 128), F32),
        V((15, 16, 128), F32),
        V((2, 4, 128), F32),
        V((NZ, LIVE, vocab), BF16),
        V((2, rows, CH), BF16),
        V((2, 2, rows // 2, CH), F32),
        V((2, rows, CH), F32),
        V((2, 2, rows // 2, CH), BF16),
        V((2, 2, 2, rows // 2, CH), BF16),
        V((2, 2, 2, rows // 2, CH), BF16),
        V((NZ, LIVE, 2 * CH), BF16),
        V((NZ - 1, LIVE, 2 * CH), BF16),
        V((NZ, LIVE, NB), F32),
        V((2, 7, LIVE, HB), BF16),
        V((2, 7, LIVE, HB), BF16),
        V((16, 8, packed), BF16),
        V((15, 8, packed), BF16),
        V((NX, 8, CH), F32),
        V((NY, 8, CH), F32),
        pltpu.SemaphoreType.DMA((4,)),
        pltpu.SemaphoreType.DMA((N_SEM,)),
        pltpu.SemaphoreType.DMA((N_SEM,)),
    ]
    grad, divergence = pl.pallas_call(
        kernel,
        out_shape=(
            jax.ShapeDtypeStruct((1, 8, width), BF16),
            jax.ShapeDtypeStruct((1, 64), F32),
        ),
        in_specs=[
            pl.BlockSpec(memory_space=pl.ANY),
            pl.BlockSpec(memory_space=pl.ANY),
            pl.BlockSpec(memory_space=pl.ANY),
            pl.BlockSpec(memory_space=pl.ANY),
        ],
        out_specs=(pl.BlockSpec(memory_space=V), pl.BlockSpec(memory_space=V)),
        scratch_shapes=scratch,
        compiler_params=pltpu.CompilerParams(
            collective_id=0, has_side_effects=True, vmem_limit_bytes=56 * 1024 * 1024
        ),
        name="distill",
    )(hidden, head_weight.reshape(width // CH, CH, vocab), teacher_logprobs, lengths.T)
    return pl.pallas_call(
        hand_over,
        out_shape=(
            jax.ShapeDtypeStruct(grad.shape, grad.dtype),
            jax.ShapeDtypeStruct(divergence.shape, divergence.dtype),
        ),
        in_specs=[pl.BlockSpec(memory_space=V)] * 2,
        out_specs=(pl.BlockSpec(memory_space=V), pl.BlockSpec(memory_space=V)),
        name="hand_over",
    )(grad, divergence)


def solution(mesh):
    placed = (
        P("dp", "section", "tensor"),
        P("tensor", ("section", "dp")),
        P(None, "tensor", ("section", "dp")),
        P(),
    )
    return jax.shard_map(
        body,
        mesh=mesh,
        in_specs=placed,
        out_specs=(P("dp", "section", "tensor"), P("dp", "tensor")),
        check_vma=False,
    )
```

time: 1590 us -> 85.6 us (0.05)
  the two profiles are of different devices: /device:TPU:0 before, /device:TPU:1 now
where the time goes in v5:
time: 85.6 us; the launch traced here: 85.5 us
  Pallas kernels  84.8 us (99%)
    pallas_call x1, Pallas kernels, body(): pl.pallas_call(kernel, out_shape=(jax.ShapeDtypeStruct((1, 8, width), BF1...  83.5 us

profile of v5, /device:TPU:1, one launch (start us, length us, event | category | flops | bytes accessed | tf_op | source)
XLA Modules:
  0.0 85.5 jit_solution(8758526426965508101)
XLA Ops:
  0.6 83.5 %distill.1 = (bf16[1,8,1792]{2,1,0:T(8,128)(2,1)}, f32[1,64]{1,0:T(1,128)}) custom-call(bf16[1,8,1792]{2,1,0:T(8,128)(2,1)} %hid_hbm.1, bf16[14,128,640]{2,1,0:T(8,128)(2,1)} %bitcast.2, f32[8,64,640]{2,1,0:T(8,128)} %tl_hbm.1, s32[4,8]{1,0:T(4,128)} %bitcast.3), custom_call_target="tpu_custom_call" | custom-call | tf_op jit(solution)/shard_map/distill/pallas_call | solution.py:405
  84.1 1.4 %hand_over.1 = (bf16[1,8,1792]{2,1,0:T(8,128)(2,1)}, f32[1,64]{1,0:T(1,128)}) custom-call(bf16[1,8,1792]{2,1,0:T(8,128)(2,1)} %get-tuple-element.4.grad_ref, f32[1,64]{1,0:T(1,128)} %get-tuple-element.5.div_ref), custom_call_target="tpu_custom_call" | custom-call | tf_op jit(solution)/shard_map/hand_over/pallas_call | solution.py:424

commit v6 on v3

--- a/solution.py
+++ b/solution.py
@@ -5,15 +5,16 @@
 from jax.experimental.pallas import tpu as pltpu
 from jax.sharding import PartitionSpec as P
 
-SEQ_MB = 32
+SEQ_MB, LIVE = 32, 80
 NX, NY, NZ = 4, 4, 8
 NA, NB = 512, 768
+HB = NB // 2
 F32, BF16 = jnp.float32, jnp.bfloat16
 
 
 def kernel(
     hid_hbm, w_hbm, tl_hbm, len_hbm, grad_ref, div_ref,
-    w, tl, tp, lengths, zb, pb, hb, bz, acc, lrecv, stats, rz, rp, g,
+    w, tl, tp, lengths, zb, pb, hb, hz, acc, lrecv, stats, rz, rp, g,
     s1, f1, own1, r1h, r1f, s2, r2, u, s3, r3, prod, sb, rb, s4, r4,
     lsem, ssem, rsem,
 ):
@@ -78,6 +79,28 @@
     zs = [send(zb.at[z], zb.at[z], at_z(k)) for k in far_z]
     ps = [send(pb.at[section], pb.at[section], at_p(k)) for k in far_p]
     acc[...] = jnp.zeros_like(acc)
+    loads[1].wait()
+
+    def position(r, j):
+        e1 = lengths[0, r]
+        e2 = e1 + lengths[1, r]
+        e3 = e2 + lengths[2, r]
+        late = jnp.where(j >= e3, 3 * SEQ_MB - e3, 2 * SEQ_MB - e2)
+        early = jnp.where(j >= e1, SEQ_MB - e1, 0)
+        return j + jnp.where(j >= e2, late, early)
+
+    def picked(r, rows):
+        j = lax.broadcasted_iota(jnp.int32, (LIVE, 128), 0)
+        p = lax.broadcasted_iota(jnp.int32, (LIVE, 128), 1)
+        pick = (p == position(r, j)).astype(F32).astype(BF16)
+        return jnp.dot(pick, rows, preferred_element_type=F32).astype(BF16)
+
+    def put_back(r, rows):
+        p = lax.broadcasted_iota(jnp.int32, (128, LIVE), 0)
+        j = lax.broadcasted_iota(jnp.int32, (128, LIVE), 1)
+        place = (p == position(r, j)).astype(F32).astype(BF16)
+        return jnp.dot(place, rows, preferred_element_type=F32)
+
     for copy in zs:
         copy.wait_recv()
     hb[x, y] = zb[...].astype(F32).reshape(NZ * 8, wide).astype(BF16)
@@ -87,24 +110,22 @@
         ph2.append(send(hb.at[x, y, :, cc], hb.at[x, y, :, cc], at_x(k)))
     for copy in ps:
         copy.wait_recv()
-    bz[z] = pb[...].astype(F32).reshape(128, NB).astype(BF16)
-
-    top_half, low_half = pl.ds(0, 64), pl.ds(64, 64)
-
-    def b_pass(step, right, rows):
-        block = bz.at[(z - step) % NZ if right else (z + step) % NZ, rows]
-        return send(block, block, at_z(1 if right else NZ - 1))
-
-    ring = [[b_pass(0, True, top_half), b_pass(0, False, low_half), b_pass(0, True, low_half), b_pass(0, False, top_half)]]
-
-    def b_forward(step, which):
-        ring[step - 1][which].wait_recv()
-        right = which in (0, 2)
-        ring[step].append(b_pass(step, right, top_half if which in (0, 3) else low_half))
-
-    ring.append([])
-    for which in range(4):
-        b_forward(1, which)
+    hz[z] = picked(z, pb[...].astype(F32).reshape(128, NB).astype(BF16))
+
+    def b_pass(step, right):
+        i = (z - step) % NZ if right else (z + step) % NZ
+        part = hz.at[i] if step < 3 else hz.at[i, :, pl.ds(0 if right else HB, HB)]
+        return send(part, part, at_z(1 if right else NZ - 1))
+
+    ring = [(b_pass(0, True), b_pass(0, False))]
+
+    def b_forward(step):
+        ring[step - 1][0].wait_recv()
+        right = b_pass(step, True)
+        ring[step - 1][1].wait_recv()
+        ring.append((right, b_pass(step, False)))
+
+    b_forward(1)
 
     for copy in ph2:
         copy.wait_recv()
@@ -137,10 +158,11 @@
         acc[:, i] = acc[:, i] + block.reshape(4, 8, 8, vocab)
 
     def b_logits(i):
-        block = jnp.dot(bz[i], w[wide:], preferred_element_type=F32)
+        rows = put_back(i, hz[i]).astype(BF16)
+        block = jnp.dot(rows, w[wide:], preferred_element_type=F32)
         acc[:, :, i] = acc[:, :, i] + block.reshape(4, 4, 8, vocab)
 
-    for load in loads:
+    for load in [loads[0]] + loads[2:]:
         load.wait()
 
     def teacher_block(k, carry):
@@ -152,9 +174,7 @@
     a_logits(x)
     c_logits(y)
 
-    ring.append([])
-    for which in range(4):
-        b_forward(2, which)
+    b_forward(2)
     b_logits((z + 1) % NZ)
     b_logits((z + 7) % NZ)
     ar0.wait_recv()
@@ -165,9 +185,7 @@
     al2 = send(a_block(x1, hi2), a_block(x1, hi2), at_x(3))
     bl0.wait_recv()
     bl2 = send(c_block(y1, hi2), c_block(y1, hi2), at_y(3))
-    ring.append([])
-    for which in range(2):
-        b_forward(3, which)
+    b_forward(3)
     b_logits((z + 2) % NZ)
     b_logits((z + 6) % NZ)
     for copy in [ar1, br1, al1, bl1]:
@@ -175,8 +193,6 @@
     for k in (1, 3):
         a_logits((x + k) % NX)
         c_logits((y + k) % NY)
-    for copy in ring[2][2:4]:
-        copy.wait_recv()
     b_logits((z + 3) % NZ)
     b_logits((z + 5) % NZ)
     for copy in (ar2, al2):
@@ -285,17 +301,17 @@
     def b_product(o):
         i = (z + o) % NZ
         rows = g[:, :, i].astype(F32).reshape(128, vocab).astype(BF16)
-        prod[i] = times_w(rows, wide, NB)
+        prod[i] = times_w(picked(i, rows), wide, NB)
 
     first = (at_x, at_y)
     second = (at_y, at_x)
-    halves = (slice(0, 64), slice(64, 128))
+    halves = (slice(0, HB), slice(HB, NB))
 
     def b_item(side, item, extra=None):
         step = 0 if item == 0 else (item + 1) // 2
         upper = (item % 2 == 0) if side == 0 else (item % 2 == 1)
         owner = (z + 4 - step) % NZ if side == 0 else (z + 4 + step) % NZ
-        value = prod[owner, halves[0 if upper else 1]]
+        value = prod[owner, :, halves[0 if upper else 1]]
         if extra is not None:
             value = value + extra
         sb[side, item] = value.astype(BF16)
@@ -371,9 +387,10 @@
     for side in range(2):
         for item in (5, 6):
             sides[side][item].wait_recv()
-    prod[z, halves[0]] = prod[z, halves[0]] + rb[0, 6].astype(F32) + rb[1, 5].astype(F32)
-    prod[z, halves[1]] = prod[z, halves[1]] + rb[0, 5].astype(F32) + rb[1, 6].astype(F32)
-    s4[...] = prod[z].reshape(16, 8, NB).astype(BF16)
+    b_first = prod[z, :, halves[0]] + rb[0, 6].astype(F32) + rb[1, 5].astype(F32)
+    b_second = prod[z, :, halves[1]] + rb[0, 5].astype(F32) + rb[1, 6].astype(F32)
+    live_rows = jnp.concatenate([b_first.astype(BF16), b_second.astype(BF16)], axis=1)
+    s4[...] = put_back(z, live_rows).reshape(16, 8, NB).astype(BF16)
     ps = [send(s4.at[plane(k)], r4.at[k - 1], at_p(k)) for k in far_p]
     for copy in zs:
         copy.wait_recv()
@@ -383,7 +400,7 @@
     grad_ref[0, :, 0:wide] = total.astype(BF16)
     for copy in ps:
         copy.wait_recv()
-    total = prod[z, pl.ds(pl.multiple_of(8 * section, 8), 8)]
+    total = s4[section].astype(F32)
     for k in range(15):
         total = total + r4[k].astype(F32)
     grad_ref[0, :, wide:] = total.astype(BF16)
@@ -412,7 +429,7 @@
         V((NZ, 8, wide), BF16),
         V((16, 8, NB), BF16),
         V((NX, NY, 64, wide), BF16),
-        V((NZ, 128, NB), BF16),
+        V((NZ, LIVE, NB), BF16),
         V((NX, NY, 8, 8, vocab), F32),
         V((8, 8, 8, vocab), F32),
         V((3, 16, 128), F32),
@@ -429,9 +446,9 @@
         V((NZ, 8, wide), F32),
         V((NZ, 8, wide), BF16),
         V((NZ - 1, 8, wide), BF16),
-        V((NZ, 128, NB), F32),
-        V((2, 7, 64, NB), BF16),
-        V((2, 7, 64, NB), BF16),
+        V((NZ, LIVE, NB), F32),
+        V((2, 7, LIVE, HB), BF16),
+        V((2, 7, LIVE, HB), BF16),
         V((16, 8, NB), BF16),
         V((15, 8, NB), BF16),
         pltpu.SemaphoreType.DMA((12,)),

time: 76.1 us -> 75.7 us (level)
  the two profiles are of different devices: /device:TPU:32 before, /device:TPU:1 now
where the time goes in v6:
time: 75.7 us; the launch traced here: 75.5 us
  Pallas kernels  74.9 us (99%)
    pallas_call x1, Pallas kernels, body(): pl.pallas_call(kernel, out_shape=(jax.ShapeDtypeStruct((1, 8, width), BF1...  73.5 us

profile of v6, /device:TPU:1, one launch (start us, length us, event | category | flops | bytes accessed | tf_op | source)
XLA Modules:
  0.0 75.5 jit_solution(16553524118243622808)
XLA Ops:
  0.6 73.5 %distill.1 = (bf16[1,8,1792]{2,1,0:T(8,128)(2,1)}, f32[1,64]{1,0:T(1,128)}) custom-call(bf16[1,8,1792]{2,1,0:T(8,128)(2,1)} %hid_hbm.1, bf16[1792,640]{1,0:T(8,128)(2,1)} %w_hbm.1, f32[8,64,640]{2,1,0:T(8,128)} %tl_hbm.1, s32[4,8]{1,0:T(4,128)} %bitcast.1), custom_call_target="tpu_custom_call" | custom-call | tf_op jit(solution)/shard_map/distill/pallas_call | solution.py:458
  74.2 1.4 %hand_over.1 = (bf16[1,8,1792]{2,1,0:T(8,128)(2,1)}, f32[1,64]{1,0:T(1,128)}) custom-call(bf16[1,8,1792]{2,1,0:T(8,128)(2,1)} %get-tuple-element.4.grad_ref, f32[1,64]{1,0:T(1,128)} %get-tuple-element.5.div_ref), custom_call_target="tpu_custom_call" | custom-call | tf_op jit(solution)/shard_map/hand_over/pallas_call | solution.py:477

commit v7 on v4

--- a/solution.py
+++ b/solution.py
@@ -5,15 +5,16 @@
 from jax.experimental.pallas import tpu as pltpu
 from jax.sharding import PartitionSpec as P
 
-SEQ_MB = 32
+SEQ_MB, LIVE = 32, 80
 NX, NY, NZ = 4, 4, 8
-NA, NC, NB = 640, 512, 640
+NA, NC, NB = 512, 512, 768
+HB = NB // 2
 F32, BF16 = jnp.float32, jnp.bfloat16
 
 
 def kernel(
     hid_hbm, w_hbm, tl_hbm, len_hbm, grad_ref, div_ref,
-    w, tl, tp, lengths, zb, pb, hb, bz, acc, lrecv, stats, rz, rp, g,
+    w, tl, tp, lengths, zb, pb, hb, hz, acc, lrecv, stats, rz, rp, g,
     s1, f1, own1, r1h, sd, r1f, s2, r2, u, s3, r3, prod, sb, rb, s4, r4,
     lsem, ssem, rsem,
 ):
@@ -78,6 +79,28 @@
     zs = [send(zb.at[z], zb.at[z], at_z(k)) for k in far_z]
     ps = [send(pb.at[section], pb.at[section], at_p(k)) for k in far_p]
     acc[...] = jnp.zeros_like(acc)
+    loads[1].wait()
+
+    def position(r, j):
+        e1 = lengths[0, r]
+        e2 = e1 + lengths[1, r]
+        e3 = e2 + lengths[2, r]
+        late = jnp.where(j >= e3, 3 * SEQ_MB - e3, 2 * SEQ_MB - e2)
+        early = jnp.where(j >= e1, SEQ_MB - e1, 0)
+        return j + jnp.where(j >= e2, late, early)
+
+    def picked(r, rows):
+        j = lax.broadcasted_iota(jnp.int32, (LIVE, 128), 0)
+        p = lax.broadcasted_iota(jnp.int32, (LIVE, 128), 1)
+        pick = (p == position(r, j)).astype(F32).astype(BF16)
+        return jnp.dot(pick, rows, preferred_element_type=F32).astype(BF16)
+
+    def put_back(r, rows):
+        p = lax.broadcasted_iota(jnp.int32, (128, LIVE), 0)
+        j = lax.broadcasted_iota(jnp.int32, (128, LIVE), 1)
+        place = (p == position(r, j)).astype(F32).astype(BF16)
+        return jnp.dot(place, rows, preferred_element_type=F32)
+
     for copy in zs:
         copy.wait_recv()
     hb[x, y] = zb[...].astype(F32).reshape(NZ * 8, wide).astype(BF16)
@@ -116,28 +139,26 @@
         send_near(part, 0)
     for copy in ps:
         copy.wait_recv()
-    bz[z] = pb[...].astype(F32).reshape(128, NB).astype(BF16)
-
-    top_half, low_half = pl.ds(0, 64), pl.ds(64, 64)
-
-    def b_pass(step, right, rows):
-        block = bz.at[(z - step) % NZ if right else (z + step) % NZ, rows]
-        return send(block, block, at_z(1 if right else NZ - 1))
-
-    ring = [[b_pass(0, True, top_half), b_pass(0, False, low_half), b_pass(0, True, low_half), b_pass(0, False, top_half)]]
-
-    def b_forward(step, which):
-        ring[step - 1][which].wait_recv()
-        right = which in (0, 2)
-        ring[step].append(b_pass(step, right, top_half if which in (0, 3) else low_half))
+    hz[z] = picked(z, pb[...].astype(F32).reshape(128, NB).astype(BF16))
+
+    def b_pass(step, right):
+        i = (z - step) % NZ if right else (z + step) % NZ
+        part = hz.at[i] if step < 3 else hz.at[i, :, pl.ds(0 if right else HB, HB)]
+        return send(part, part, at_z(1 if right else NZ - 1))
+
+    ring = [(b_pass(0, True), b_pass(0, False))]
+
+    def b_forward(step):
+        ring[step - 1][0].wait_recv()
+        right = b_pass(step, True)
+        ring[step - 1][1].wait_recv()
+        ring.append((right, b_pass(step, False)))
 
     for k in (1, 3):
         for part in range(2):
             spread[part, k].wait_recv()
             send_near(part, 4 - k)
-    ring.append([])
-    for which in range(4):
-        b_forward(1, which)
+    b_forward(1)
     for part in range(2):
         spread[part, 2].wait_recv()
         send_near(part, 2)
@@ -154,7 +175,8 @@
         acc[:, i] = acc[:, i] + block.reshape(4, 8, 8, vocab)
 
     def b_logits(i):
-        block = jnp.dot(bz[i], w[wide:], preferred_element_type=F32)
+        rows = put_back(i, hz[i]).astype(BF16)
+        block = jnp.dot(rows, w[wide:], preferred_element_type=F32)
         acc[:, :, i] = acc[:, :, i] + block.reshape(4, 4, 8, vocab)
 
     def c_far(owner):
@@ -163,13 +185,7 @@
         into = acc.at[pl.ds(2 * owner, 2), (y + 2) % NY]
         into[...] = into[...] + block.reshape(2, 8, 8, vocab)
 
-    def b_far(owner):
-        rows = bz[(z + 4) % NZ, pl.ds(pl.multiple_of(64 * owner, 64), 64), :]
-        block = jnp.dot(rows, w[wide:], preferred_element_type=F32)
-        into = acc.at[pl.ds(2 * owner, 2), :, (z + 4) % NZ]
-        into[...] = into[...] + block.reshape(2, 4, 8, vocab)
-
-    for load in loads:
+    for load in [loads[0]] + loads[2:]:
         load.wait()
 
     def teacher_block(k, carry):
@@ -183,9 +199,7 @@
     for k in (1, 3):
         for part in range(2):
             pass_on(part, k)
-    ring.append([])
-    for which in range(4):
-        b_forward(2, which)
+    b_forward(2)
     b_logits((z + 1) % NZ)
     b_logits((z + 7) % NZ)
     for part in range(2):
@@ -193,13 +207,9 @@
     for k in (1, 3):
         a_logits((x + k) % NX)
         c_logits((y + k) % NY)
-    ring.append([])
-    for which in range(2):
-        b_forward(3, which)
+    b_forward(3)
     b_logits((z + 2) % NZ)
     b_logits((z + 6) % NZ)
-    for copy in ring[2][2:4]:
-        copy.wait_recv()
     b_logits((z + 3) % NZ)
     b_logits((z + 5) % NZ)
     for k in range(4):
@@ -209,14 +219,13 @@
         passed[1, k].wait_recv()
     for copy in ring[3]:
         copy.wait_recv()
+    b_logits((z + 4) % NZ)
     c_far(other)
-    b_far(other)
     exchanges = []
     for k in range(4):
         block = acc.at[2 * other + k // 2, pl.ds(2 * (k % 2), 2)]
         exchanges.append(send(block, lrecv.at[pl.ds(2 * k, 2)], partner))
     c_far(t)
-    b_far(t)
 
     row_i = lax.broadcasted_iota(jnp.int32, (128, 128), 0)
     lane_i = lax.broadcasted_iota(jnp.int32, (128, 128), 1)
@@ -310,19 +319,19 @@
     def b_product(o):
         i = (z + o) % NZ
         rows = g[:, :, i].astype(F32).reshape(128, vocab).astype(BF16)
-        prod[i] = times_w(rows, wide, NB)
+        prod[i] = times_w(picked(i, rows), wide, NB)
 
     size = (NA, NC)
     fit = (pl.ds(0, NA), pl.ds(0, NC))
     mine = (y, x)
     order = (2, 1, 3, 0)
-    halves = (slice(0, 64), slice(64, 128))
+    halves = (slice(0, HB), slice(HB, NB))
 
     def b_item(side, item, extra=None):
         step = 0 if item == 0 else (item + 1) // 2
         upper = (item % 2 == 0) if side == 0 else (item % 2 == 1)
         owner = (z + 4 - step) % NZ if side == 0 else (z + 4 + step) % NZ
-        value = prod[owner, halves[0 if upper else 1]]
+        value = prod[owner, :, halves[0 if upper else 1]]
         if extra is not None:
             value = value + extra
         sb[side, item] = value.astype(BF16)
@@ -412,9 +421,10 @@
     for side in range(2):
         for item in (5, 6):
             sides[side][item].wait_recv()
-    prod[z, halves[0]] = prod[z, halves[0]] + rb[0, 6].astype(F32) + rb[1, 5].astype(F32)
-    prod[z, halves[1]] = prod[z, halves[1]] + rb[0, 5].astype(F32) + rb[1, 6].astype(F32)
-    s4[...] = prod[z].reshape(16, 8, NB).astype(BF16)
+    b_first = prod[z, :, halves[0]] + rb[0, 6].astype(F32) + rb[1, 5].astype(F32)
+    b_second = prod[z, :, halves[1]] + rb[0, 5].astype(F32) + rb[1, 6].astype(F32)
+    live_rows = jnp.concatenate([b_first.astype(BF16), b_second.astype(BF16)], axis=1)
+    s4[...] = put_back(z, live_rows).reshape(16, 8, NB).astype(BF16)
     ps = [send(s4.at[plane(k)], r4.at[k - 1], at_p(k)) for k in far_p]
     for copy in zs:
         copy.wait_recv()
@@ -424,7 +434,7 @@
     grad_ref[0, :, 0:wide] = total.astype(BF16)
     for copy in ps:
         copy.wait_recv()
-    total = prod[z, pl.ds(pl.multiple_of(8 * section, 8), 8)]
+    total = s4[section].astype(F32)
     for k in range(15):
         total = total + r4[k].astype(F32)
     grad_ref[0, :, wide:] = total.astype(BF16)
@@ -453,7 +463,7 @@
         V((NZ, 8, wide), BF16),
         V((16, 8, NB), BF16),
         V((NX, NY, 64, wide), BF16),
-        V((NZ, 128, NB), BF16),
+        V((NZ, LIVE, NB), BF16),
         V((NX, NY, 8, 8, vocab), F32),
         V((8, 8, 8, vocab), F32),
         V((3, 16, 128), F32),
@@ -471,9 +481,9 @@
         V((NZ, 8, wide), F32),
         V((NZ, 8, wide), BF16),
         V((NZ - 1, 8, wide), BF16),
-        V((NZ, 128, NB), F32),
-        V((2, 7, 64, NB), BF16),
-        V((2, 7, 64, NB), BF16),
+        V((NZ, LIVE, NB), F32),
+        V((2, 7, LIVE, HB), BF16),
+        V((2, 7, LIVE, HB), BF16),
         V((16, 8, NB), BF16),
         V((15, 8, NB), BF16),
         pltpu.SemaphoreType.DMA((12,)),

time: 77.9 us -> 75.9 us (0.974); the launches traced: 77.7 us -> 74.9 us
  Pallas kernels: 77.1 us -> 74.3 us
    pallas_call x1, Pallas kernels: 75.7 us -> 72.9 us  [body(): pl.pallas_call(kernel, out_shape=(jax.ShapeDtypeStruct((1, 8, width), BF1...]
where the time goes in v7:
time: 75.9 us; the launch traced here: 74.9 us
  Pallas kernels  74.3 us (98%)
    pallas_call x1, Pallas kernels, body(): pl.pallas_call(kernel, out_shape=(jax.ShapeDtypeStruct((1, 8, width), BF1...  72.9 us

profile of v7, /device:TPU:1, one launch (start us, length us, event | category | flops | bytes accessed | tf_op | source)
XLA Modules:
  0.0 74.9 jit_solution(7333225212308466988)
XLA Ops:
  0.6 72.9 %distill.1 = (bf16[1,8,1792]{2,1,0:T(8,128)(2,1)}, f32[1,64]{1,0:T(1,128)}) custom-call(bf16[1,8,1792]{2,1,0:T(8,128)(2,1)} %hid_hbm.1, bf16[1792,640]{1,0:T(8,128)(2,1)} %w_hbm.1, f32[8,64,640]{2,1,0:T(8,128)} %tl_hbm.1, s32[4,8]{1,0:T(4,128)} %bitcast.1), custom_call_target="tpu_custom_call" | custom-call | tf_op jit(solution)/shard_map/distill/pallas_call | solution.py:493
  73.6 1.4 %hand_over.1 = (bf16[1,8,1792]{2,1,0:T(8,128)(2,1)}, f32[1,64]{1,0:T(1,128)}) custom-call(bf16[1,8,1792]{2,1,0:T(8,128)(2,1)} %get-tuple-element.4.grad_ref, f32[1,64]{1,0:T(1,128)} %get-tuple-element.5.div_ref), custom_call_target="tpu_custom_call" | custom-call | tf_op jit(solution)/shard_map/hand_over/pallas_call | solution.py:512

commit v8 on v6

--- a/solution.py
+++ b/solution.py
@@ -161,6 +161,12 @@
         rows = put_back(i, hz[i]).astype(BF16)
         block = jnp.dot(rows, w[wide:], preferred_element_type=F32)
         acc[:, :, i] = acc[:, :, i] + block.reshape(4, 4, 8, vocab)
+
+    def c_far(owner):
+        rows = hb[pl.ds(2 * owner, 2), (y + 2) % NY, :, NA:wide].reshape(128, NA)
+        block = jnp.dot(rows, w[NA:wide], preferred_element_type=F32)
+        into = acc.at[pl.ds(2 * owner, 2), (y + 2) % NY]
+        into[...] = into[...] + block.reshape(2, 8, 8, vocab)
 
     for load in [loads[0]] + loads[2:]:
         load.wait()
@@ -195,19 +201,20 @@
         c_logits((y + k) % NY)
     b_logits((z + 3) % NZ)
     b_logits((z + 5) % NZ)
+    for copy in ring[3]:
+        copy.wait_recv()
+    b_logits((z + 4) % NZ)
     for copy in (ar2, al2):
         copy.wait_recv()
     a_logits((x + 2) % NX)
     for copy in (br2, bl2):
         copy.wait_recv()
-    c_logits((y + 2) % NY)
-    for copy in ring[3]:
-        copy.wait_recv()
-    b_logits((z + 4) % NZ)
+    c_far(other)
     exchanges = []
     for k in range(4):
         block = acc.at[2 * other + k // 2, pl.ds(2 * (k % 2), 2)]
         exchanges.append(send(block, lrecv.at[pl.ds(2 * k, 2)], partner))
+    c_far(t)
 
     row_i = lax.broadcasted_iota(jnp.int32, (128, 128), 0)
     lane_i = lax.broadcasted_iota(jnp.int32, (128, 128), 1)
@@ -318,18 +325,14 @@
         return send(sb.at[side, item], rb.at[side, item], at_z(1 if side == 0 else NZ - 1))
 
     hop, direct = [], []
-    b_product(4)
-    sides = [[b_item(side, 0)] for side in range(2)]
     for part in range(2):
         s1[part, 2] = product(part, 2).astype(BF16)
         hop.append((
             send(s1.at[part, 2, lo2], r1h.at[part, 0], first[part](1)),
             send(s1.at[part, 2, hi2], r1h.at[part, 1], first[part](3)),
         ))
-    for side in range(2):
-        b_product((3, 5)[side])
-        sides[side].append(b_item(side, 1))
-
+    b_product(4)
+    sides = [[b_item(side, 0)] for side in range(2)]
     def b_next(item):
         source = 0 if item == 2 else item - 2
         for side in range(2):
@@ -345,6 +348,9 @@
         f1[part, 1] = block[2:4]
         s1[part, 3, 0:2] = block[0:2].astype(BF16)
         direct.append(send(s1.at[part, 3, lo2], r1f.at[part, 1, lo2], first[part](3)))
+    for side in range(2):
+        b_product((3, 5)[side])
+        sides[side].append(b_item(side, 1))
     b_next(2)
     b_product(2)
     b_product(6)

time: 75.7 us -> 75.2 us (level)
  Pallas kernels: 74.9 us -> 74 us
    pallas_call x1, Pallas kernels: 73.5 us -> 72.6 us  [body(): pl.pallas_call(kernel, out_shape=(jax.ShapeDtypeStruct((1, 8, width), BF1...]
where the time goes in v8:
time: 75.2 us; the launch traced here: 74.6 us
  Pallas kernels  74 us (98%)
    pallas_call x1, Pallas kernels, body(): pl.pallas_call(kernel, out_shape=(jax.ShapeDtypeStruct((1, 8, width), BF1...  72.6 us

profile of v8, /device:TPU:1, one launch (start us, length us, event | category | flops | bytes accessed | tf_op | source)
XLA Modules:
  0.0 74.6 jit_solution(16747533168912974782)
XLA Ops:
  0.6 72.6 %distill.1 = (bf16[1,8,1792]{2,1,0:T(8,128)(2,1)}, f32[1,64]{1,0:T(1,128)}) custom-call(bf16[1,8,1792]{2,1,0:T(8,128)(2,1)} %hid_hbm.1, bf16[1792,640]{1,0:T(8,128)(2,1)} %w_hbm.1, f32[8,64,640]{2,1,0:T(8,128)} %tl_hbm.1, s32[4,8]{1,0:T(4,128)} %bitcast.1), custom_call_target="tpu_custom_call" | custom-call | tf_op jit(solution)/shard_map/distill/pallas_call | solution.py:464
  73.2 1.4 %hand_over.1 = (bf16[1,8,1792]{2,1,0:T(8,128)(2,1)}, f32[1,64]{1,0:T(1,128)}) custom-call(bf16[1,8,1792]{2,1,0:T(8,128)(2,1)} %get-tuple-element.4.grad_ref, f32[1,64]{1,0:T(1,128)} %get-tuple-element.5.div_ref), custom_call_target="tpu_custom_call" | custom-call | tf_op jit(solution)/shard_map/hand_over/pallas_call | solution.py:483

commit v9 on v8

--- a/solution.py
+++ b/solution.py
@@ -15,7 +15,7 @@
 def kernel(
     hid_hbm, w_hbm, tl_hbm, len_hbm, grad_ref, div_ref,
     w, tl, tp, lengths, zb, pb, hb, hz, acc, lrecv, stats, rz, rp, g,
-    s1, f1, own1, r1h, r1f, s2, r2, u, s3, r3, prod, sb, rb, s4, r4,
+    s1, own1, r1f, s2, r2, u, s3, r3, prod, sb, rb, s4, r4,
     lsem, ssem, rsem,
 ):
     wide = NA + NA
@@ -324,13 +324,14 @@
         sb[side, item] = value.astype(BF16)
         return send(sb.at[side, item], rb.at[side, item], at_z(1 if side == 0 else NZ - 1))
 
-    hop, direct = [], []
-    for part in range(2):
-        s1[part, 2] = product(part, 2).astype(BF16)
-        hop.append((
-            send(s1.at[part, 2, lo2], r1h.at[part, 0], first[part](1)),
-            send(s1.at[part, 2, hi2], r1h.at[part, 1], first[part](3)),
-        ))
+    direct = []
+
+    def direct_sum(o):
+        for part in range(2):
+            s1[part, o - 1] = product(part, o).astype(BF16)
+            direct.append(send(s1.at[part, o - 1], r1f.at[part, o - 1], first[part](o)))
+
+    direct_sum(2)
     b_product(4)
     sides = [[b_item(side, 0)] for side in range(2)]
     def b_next(item):
@@ -339,28 +340,14 @@
             sides[side][source].wait_recv()
             sides[side].append(b_item(side, item, rb[side, source].astype(F32)))
 
-    for part in range(2):
-        block = product(part, 1)
-        f1[part, 0] = block[0:2]
-        s1[part, 1, 2:4] = block[2:4].astype(BF16)
-        direct.append(send(s1.at[part, 1, hi2], r1f.at[part, 0, hi2], first[part](1)))
-        block = product(part, 3)
-        f1[part, 1] = block[2:4]
-        s1[part, 3, 0:2] = block[0:2].astype(BF16)
-        direct.append(send(s1.at[part, 3, lo2], r1f.at[part, 1, lo2], first[part](3)))
+    direct_sum(1)
+    direct_sum(3)
     for side in range(2):
         b_product((3, 5)[side])
         sides[side].append(b_item(side, 1))
     b_next(2)
     b_product(2)
     b_product(6)
-    for part in range(2):
-        hop[part][0].wait_recv()
-        s1[part, 1, 0:2] = (f1[part, 0] + r1h[part, 0].astype(F32)).astype(BF16)
-        direct.append(send(s1.at[part, 1, lo2], r1f.at[part, 0, lo2], first[part](1)))
-        hop[part][1].wait_recv()
-        s1[part, 3, 2:4] = (f1[part, 1] + r1h[part, 1].astype(F32)).astype(BF16)
-        direct.append(send(s1.at[part, 3, hi2], r1f.at[part, 1, hi2], first[part](3)))
     b_next(3)
     b_product(1)
     b_product(7)
@@ -376,7 +363,7 @@
     for k in (2, 1, 3):
         for part in range(2):
             i = (place2[part] + k) % 4
-            value = own1[part, i] + r1f[part, 0, i].astype(F32) + r1f[part, 1, i].astype(F32)
+            value = own1[part, i] + sum(r1f[part, j, i].astype(F32) for j in range(3))
             s2[part, k - 1] = value.astype(BF16)
             ph2.append(send(s2.at[part, k - 1], r2.at[part, k - 1], second[part](k)))
     b_next(6)
@@ -384,7 +371,7 @@
         copy.wait_recv()
     for part in range(2):
         i = place2[part]
-        value = own1[part, i] + r1f[part, 0, i].astype(F32) + r1f[part, 1, i].astype(F32)
+        value = own1[part, i] + sum(r1f[part, j, i].astype(F32) for j in range(3))
         for k in range(3):
             value = value + r2[part, k].astype(F32)
         u[:, :, part * NA:(part + 1) * NA] = value.reshape(NZ, 8, NA)
@@ -442,11 +429,9 @@
         V((NZ - 1, 16, 128), F32),
         V((15, 16, 128), F32),
         V((NX, NY, 8, 8, vocab), BF16),
-        V((2, 4, 4, 64, NA), BF16),
-        V((2, 2, 2, 64, NA), F32),
+        V((2, 3, 4, 64, NA), BF16),
         V((2, 4, 64, NA), F32),
-        V((2, 2, 2, 64, NA), BF16),
-        V((2, 2, 4, 64, NA), BF16),
+        V((2, 3, 4, 64, NA), BF16),
         V((2, 3, 64, NA), BF16),
         V((2, 3, 64, NA), BF16),
         V((NZ, 8, wide), F32),

time: 75.2 us -> 78.9 us (1.049)
  Pallas kernels: 74 us -> 78.1 us
    pallas_call x1, Pallas kernels: 72.6 us -> 76.7 us  [body(): pl.pallas_call(kernel, out_shape=(jax.ShapeDtypeStruct((1, 8, width), BF1...]
where the time goes in v9:
time: 78.9 us; the launch traced here: 78.7 us
  Pallas kernels  78.1 us (99%)
    pallas_call x1, Pallas kernels, body(): pl.pallas_call(kernel, out_shape=(jax.ShapeDtypeStruct((1, 8, width), BF1...  76.7 us

profile of v9, /device:TPU:1, one launch (start us, length us, event | category | flops | bytes accessed | tf_op | source)
XLA Modules:
  0.0 78.7 jit_solution(13538381935180842406)
XLA Ops:
  0.6 76.7 %distill.1 = (bf16[1,8,1792]{2,1,0:T(8,128)(2,1)}, f32[1,64]{1,0:T(1,128)}) custom-call(bf16[1,8,1792]{2,1,0:T(8,128)(2,1)} %hid_hbm.1, bf16[1792,640]{1,0:T(8,128)(2,1)} %w_hbm.1, f32[8,64,640]{2,1,0:T(8,128)} %tl_hbm.1, s32[4,8]{1,0:T(4,128)} %bitcast.1), custom_call_target="tpu_custom_call" | custom-call | tf_op jit(solution)/shard_map/distill/pallas_call | solution.py:449
  77.4 1.4 %hand_over.1 = (bf16[1,8,1792]{2,1,0:T(8,128)(2,1)}, f32[1,64]{1,0:T(1,128)}) custom-call(bf16[1,8,1792]{2,1,0:T(8,128)(2,1)} %get-tuple-element.4.grad_ref, f32[1,64]{1,0:T(1,128)} %get-tuple-element.5.div_ref), custom_call_target="tpu_custom_call" | custom-call | tf_op jit(solution)/shard_map/hand_over/pallas_call | solution.py:468
